TPU v7x, 512 devices: a whole 4x4x16 slice. The times are simulated.
512 devices in a mesh: tile: 128 (over y_lo, x, z), dir: 4 (over y_hi, core).
Axes of the slice: x: 4, y: 4 (y_hi: 2, y_lo: 2; y = y_hi * 2 + y_lo), z: 16, core: 2. Of those that a mesh axis runs over, the one named last changes fastest.
Arguments:
- layers: bfloat16 [4, 16384, 2048], P('dir', 'tile'), may hold values from -6 to 6
- offsets: int32 [4, 4, 2], replicated, may hold values from 0 to 8191, as said below
- subap_valid: int32 [128, 16], P('tile'), may hold values from 0 to 1, as said below
- defocus: float32 [3], replicated, may hold values from -0.08 to 0.08
- weights: float32 [3], replicated, may hold values from 0.25 to 1
Outputs:
- spots: bfloat16 [4, 128, 128, 2048], P('dir', 'tile')
Inputs may be any that keep to these rules, and one draw needn't show every extreme that they name: offsets[d, l, 0] < 1024 and offsets[d, l, 1] < 8192; both bounds minus one are taken by some pair in every draw. `subap_valid`: the part of an annulus of lit subapertures that falls in the strip, with a few dead ones.
All inputs are finite; a program needn't handle non-finite values.
Results may differ from a plain program's by a relative error of at most 0.0055.
Values may be sent and summed in bfloat16 or wider, within the bound.
No kernel may reach another device: no remote copies, remote signals or barrier semaphores. Data moves between devices by JAX's collectives and lax.ppermute only.
A program may use at most 64 MiB of HBM per device.

v0:
```python
import math

import jax
import jax.numpy as jnp
from jax import lax
from jax.sharding import PartitionSpec as P

SUBPIX = 128
SPOT = 128
SUBX = 16
SLICES = 3
REACH = 2
QUANT = 4
OVER = 2
PCOLS = 2048


def shifted(value, axis, by):
    count = lax.axis_size(axis)
    return lax.ppermute(value, axis, [(i, (i + by) % count) for i in range(count)])


def tables():
    frequency = jnp.arange(SPOT, dtype=jnp.float32) - SPOT // 2
    position = jnp.arange(SUBPIX, dtype=jnp.float32) - (SUBPIX - 1) / 2.0
    phase_angle = -2.0 * math.pi / (OVER * SUBPIX) * frequency[:, None] * position[None, :]
    factor = 1.0 / math.sqrt(SUBPIX)
    real_part = jnp.cos(phase_angle) * factor
    imag_part = jnp.sin(phase_angle) * factor
    left_table = jnp.concatenate(
        [jnp.concatenate([real_part, -imag_part], 1), jnp.concatenate([imag_part, real_part], 1)], 0
    ).astype(jnp.bfloat16)
    right_table = jnp.concatenate(
        [
            jnp.concatenate([real_part.T, imag_part.T], 1),
            jnp.concatenate([-imag_part.T, real_part.T], 1),
        ],
        0,
    ).astype(jnp.bfloat16)
    return (left_table, right_table)


def interpolate(window, offset_pair):
    col_steps = offset_pair[1] // QUANT
    col_frac = (offset_pair[1] % QUANT).astype(jnp.float32) / QUANT
    row_frac = (offset_pair[0] % QUANT).astype(jnp.float32) / QUANT
    col_first = jnp.roll(window, -col_steps, axis=1)
    col_second = jnp.roll(window, -(col_steps + 1), axis=1)
    across = (1.0 - col_frac) * col_first + col_frac * col_second
    return ((1.0 - row_frac) * across[:-1] + row_frac * across[1:]).astype(jnp.bfloat16)


def spots_row(pupil_phase, first_row, total_rows, defocus, weights, valid_row):
    left_table, right_table = tables()
    row_position = (
        (first_row + jnp.arange(SUBPIX, dtype=jnp.int32)).astype(jnp.float32)
        - (total_rows - 1) / 2.0
    ) / SUBPIX
    col_position = (jnp.arange(PCOLS, dtype=jnp.float32) - (PCOLS - 1) / 2.0) / SUBPIX
    radius = row_position[:, None] ** 2 + col_position[None, :] ** 2
    spot_sum = jnp.zeros((SPOT * SUBX, SPOT), jnp.float32)
    for altitude in range(SLICES):
        phase_angle = pupil_phase + defocus[altitude] * radius
        pupil_field = jnp.concatenate([jnp.cos(phase_angle), jnp.sin(phase_angle)], 0).astype(
            jnp.bfloat16
        )
        focal_plane = jnp.dot(left_table, pupil_field, preferred_element_type=jnp.float32).astype(
            jnp.bfloat16
        )
        blocks = jnp.concatenate(
            [
                focal_plane[:SPOT].reshape(SPOT * SUBX, SUBPIX),
                focal_plane[SPOT:].reshape(SPOT * SUBX, SUBPIX),
            ],
            1,
        )
        spot_field = jnp.dot(blocks, right_table, preferred_element_type=jnp.float32)
        spot_sum = spot_sum + weights[altitude] * (
            spot_field[:, :SPOT] ** 2 + spot_field[:, SPOT:] ** 2
        )
    scaled = spot_sum / jnp.sum(weights)
    masked = scaled.reshape(SPOT, SUBX, SPOT) * valid_row.astype(jnp.float32)[None, :, None]
    return masked.reshape(SPOT, SUBX * SPOT).astype(jnp.bfloat16)


def extend(block):
    pieces = [block]
    for distance in range(1, REACH + 1):
        pieces.append(shifted(block, "tile", -distance))
    return jnp.concatenate(pieces, 1)


def shifted_term(extended, offset_pair):
    window = lax.dynamic_slice_in_dim(extended, offset_pair[0] // QUANT, SUBPIX + 1, 0).astype(
        jnp.float32
    )
    return interpolate(window, offset_pair)


def shards(layers, offsets, subap_valid, defocus, weights):
    own_dir = lax.axis_index("dir")
    tile_index = lax.axis_index("tile")
    total_rows = lax.axis_size("tile") * SUBPIX
    pupil_phase = jnp.zeros((SUBPIX, PCOLS), jnp.float32)
    stacked = lax.all_gather(layers, "dir", axis=0, tiled=True)
    extended = extend(stacked)
    offset_pairs = lax.dynamic_index_in_dim(offsets, own_dir, 0, keepdims=False)
    for layer_index in range(stacked.shape[0]):
        pupil_phase = pupil_phase + shifted_term(
            extended[layer_index], offset_pairs[layer_index]
        ).astype(jnp.float32)
    spots = spots_row(
        pupil_phase, tile_index * SUBPIX, total_rows, defocus, weights, subap_valid[0]
    )
    return spots[None, None]


def solution(mesh):
    placed = (P("dir", "tile", None), P(), P("tile", None), P(), P())
    return jax.shard_map(
        shards, mesh=mesh, in_specs=placed, out_specs=P("dir", "tile", None, None), check_vma=False
    )
```

profile of v0, /device:TPU:1, one launch (start us, length us, event | category | flops | bytes accessed | tf_op | source)
XLA Modules:
  0.0 236.6 jit_solution(6538307953497980572)
XLA Ops:
  6.5 0.0 copy-start
  6.5 0.0 all-gather.2.cloned.1.call-start
  6.5 0.7 all-gather.2.cloned.1.call-update
  7.3 42.3 %all-gather.2.cloned.1.call-done = bf16[4,128,2048]{2,1,0:T(8,128)(2,1)} async-done(((bf16[1,128,2048]{2,1,0:T(8,128)(2,1)}), bf16[4,128,2048]{2,1,0:T(8,128)(2,1)}) %all-gather.2.cloned.1.call-update) | async-done | bytes 2097168 | tf_op jit(solution)/shard_map/all_gather | solution.py:105
  49.5 7.8 %collective-permute-start = (bf16[4,128,2048]{2,1,0:T(8,128)(2,1)}, bf16[4,128,2048]{2,1,0:T(8,128)(2,1)}, u32[]{:S(2)}, u32[]{:S(2)}) collective-permute-start(bf16[4,128,2048]{2,1,0:T(8,128)(2,1)} %all-gather.2.cloned.1.call-done), channel_id=1, source_target_pairs={{0,508},{4,0},{8,4},{12,8},{16,12},{20,16},{24,20},{28,24},{32,28}... | collective-permute-start | bytes 6291464 | tf_op jit(solution)/shard_map/ppermute | solution.py:20
  57.4 3.8 %collective-permute-start.1 = (bf16[4,128,2048]{2,1,0:T(8,128)(2,1)}, bf16[4,128,2048]{2,1,0:T(8,128)(2,1)S(1)}, u32[]{:S(2)}, u32[]{:S(2)}) collective-permute-start(bf16[4,128,2048]{2,1,0:T(8,128)(2,1)} %all-gather.2.cloned.1.call-done), channel_id=1, source_target_pairs={{0,504},{4,508},{8,0},{12,4},{16,8},{20,12},{24,16},{28,20},{32,24... | collective-permute-start | bytes 6291464 | tf_op jit(solution)/shard_map/ppermute | solution.py:20
  61.2 0.0 copy-done
  61.2 0.7 fusion.83
  83.2 1.3 reduce_sum.9
  84.5 1.4 fusion.84
  85.9 1.4 fusion.85
  87.4 0.7 convert_bitcast_fusion
  88.0 0.1 broadcast_bitcast_fusion
  88.1 0.6 fusion.71
  88.6 1.7 constant_dynamic-update-slice_fusion.2
  90.4 18.5 %collective-permute-done = bf16[4,128,2048]{2,1,0:T(8,128)(2,1)} collective-permute-done((bf16[4,128,2048]{2,1,0:T(8,128)(2,1)}, bf16[4,128,2048]{2,1,0:T(8,128)(2,1)}, u32[]{:S(2)}, u32[]{:S(2)}) %collective-permute-start) | collective-permute-done | bytes 2097184 | tf_op jit(solution)/shard_map/ppermute | solution.py:20
  108.9 1.7 constant_dynamic-update-slice_fusion.1
  110.6 81.7 %collective-permute-done.1 = bf16[4,128,2048]{2,1,0:T(8,128)(2,1)S(1)} collective-permute-done((bf16[4,128,2048]{2,1,0:T(8,128)(2,1)}, bf16[4,128,2048]{2,1,0:T(8,128)(2,1)S(1)}, u32[]{:S(2)}, u32[]{:S(2)}) %collective-permute-start.1) | collective-permute-done | bytes 2097184 | tf_op jit(solution)/shard_map/ppermute | solution.py:20
  192.3 0.1 constant_dynamic-update-slice_fusion
  192.4 1.0 fusion.79
  193.4 0.3 bitcast_convert_fusion.2
  193.7 1.2 fusion.17
  195.0 1.2 fusion.12
  196.2 0.3 bitcast_convert_fusion
  196.6 1.2 fusion.7
  197.8 1.2 fusion.2
  199.0 5.3 %cosine_convert_fusion.2 = (bf16[128,2048]{1,0:T(8,128)(2,1)S(1)}, f32[128,2048]{1,0:T(8,128)S(1)}) fusion(f32[2048]{0:T(1024)S(1)} %multiply_multiply_fusion, f32[128]{0:T(128)S(1)} %multiply_multiply_fusion.1, f32[]{:T(128)} %bitcast.17, f32[129,2048]{1,0:T(8,128)S(1)} %fusion.2, f32[]{:T(128)S(6)} %div.123, f32[]{:T(128)S(6)} %sub.110, ...), kind=kLoop, calls=%fused_computation.103 | loop fusion | flops 7077888 | bytes 9970212 | tf_op jit(solution)/shard_map/convert.14
  204.4 13.9 %sine_convert_fusion.2 = (bf16[128,2048]{1,0:T(8,128)(2,1)S(1)}, bf16[128,2048]{1,0:T(8,128)(2,1)S(1)}, bf16[128,2048]{1,0:T(8,128)(2,1)S(1)}, bf16[128,2048]{1,0:T(8,128)(2,1)}, bf16[128,2048]{1,0:T(8,128)(2,1)S(1)}) fusion(f32[128,2048]{1,0:T(8,128)S(1)} %get-tuple-element.7, f32[2048]{0:T(1024)S(1)} %multiply_multiply_fusion, ...), kind=kLoop, calls=%fused_computation.102 | loop fusion | flops 3145728 | bytes 3678732 | tf_op jit(solution)/shard_map/convert.15
  218.3 0.4 convolution_convert_fusion.2
  218.7 0.1 fusion.80
  218.8 0.2 reshape.129
  219.0 0.2 reshape.130
  219.3 0.5 convolution_convert_fusion.1
  219.7 0.1 fusion.81
  219.9 0.2 reshape.131
  220.1 0.2 reshape.132
  220.4 1.5 convolution_convert_fusion
  221.8 0.9 fusion.82
  222.7 0.2 reshape.133
  223.0 1.3 reshape.134
  224.3 0.4 fusion.43
  224.7 0.4 fusion.50
  225.1 0.4 fusion.57
  225.6 3.1 %fusion.26 = f32[2048,128]{1,0:T(8,128)S(1)} fusion(f32[2048,256]{1,0:T(8,128)S(1)} %fusion.57, f32[2048,256]{1,0:T(8,128)S(1)} %fusion.50, f32[2048,256]{1,0:T(8,128)S(1)} %fusion.43, f32[]{:T(128)} %reduce_sum.9, f32[]{:T(128)} %bitcast.20, f32[]{:T(128)} %bitcast.18, f32[]{:T(128)} %bitcast), kind=kLoop, calls=%fused_computation.49 | loop fusion | flops 3932160 | bytes 7340048 | tf_op jit(solution)/shard_map/div | solution.py:81
  228.7 0.2 reshape.135
  228.8 0.9 multiply_convert_fusion
  (4 shorter events, 0.0 us)
Async XLA Ops:
  6.5 54.6 %copy-start = (s32[4,4,2]{1,2,0:T(2,128)S(1)}, s32[4,4,2]{1,2,0:T(2,128)}, u32[]{:S(2)}) copy-start(s32[4,4,2]{1,2,0:T(2,128)} %param.8) | copy-start | bytes 388
  6.5 43.0 %all-gather.2.cloned.1.call-start = ((), (), s32[]{:S(2)}) async-start(), calls=%async_computation | async-start | bytes 2621440 | tf_op jit(solution)/shard_map/all_gather | solution.py:105
  49.5 59.4 %collective-permute-start = (bf16[4,128,2048]{2,1,0:T(8,128)(2,1)}, bf16[4,128,2048]{2,1,0:T(8,128)(2,1)}, u32[]{:S(2)}, u32[]{:S(2)}) collective-permute-start(bf16[4,128,2048]{2,1,0:T(8,128)(2,1)} %all-gather.2.cloned.1.call-done), channel_id=1, source_target_pairs={{0,508},{4,0},{8,4},{12,8},{16,12},{20,16},{24,20},{28,24},{32,28}... | collective-permute-start | bytes 6291464 | tf_op jit(solution)/shard_map/ppermute | solution.py:20
  57.4 134.9 %collective-permute-start.1 = (bf16[4,128,2048]{2,1,0:T(8,128)(2,1)}, bf16[4,128,2048]{2,1,0:T(8,128)(2,1)S(1)}, u32[]{:S(2)}, u32[]{:S(2)}) collective-permute-start(bf16[4,128,2048]{2,1,0:T(8,128)(2,1)} %all-gather.2.cloned.1.call-done), channel_id=1, source_target_pairs={{0,504},{4,508},{8,0},{12,4},{16,8},{20,12},{24,16},{28,20},{32,24... | collective-permute-start | bytes 6291464 | tf_op jit(solution)/shard_map/ppermute | solution.py:20
Sparse Core Ops, SparseCore 0:
  9.5 40.0 all-gather.1
where the time goes:
time: 237 us
  waiting for transfers between devices  143 us (60%)
  between operations  34.9 us (15%)
  other arithmetic  31.4 us (13%)
  local copies, waits for them, and re-layouts  11.9 us (5%)
  starting transfers between devices  11.6 us (5%)
  matrix products  3.69 us (2%)
    ppermute x2, waiting for transfers between devices, shifted(): lax.ppermute(value, axis, [(i, (i + by) % count) for i in range(count)])  100 us
    all_gather x1, waiting for transfers between devices, shards(): stacked = lax.all_gather(layers, 'dir', axis=0, tiled=True)  42.3 us
    another operation x3, other arithmetic  19.8 us
    ppermute x2, starting transfers between devices, shifted(): lax.ppermute(value, axis, [(i, (i + by) % count) for i in range(count)])  11.6 us
    add x4, other arithmetic, interpolate(): across = (1.0 - col_frac) * col_first + col_frac * col_second  4.96 us
  transfers between devices with their start and end apart: 3, of which 3 were waited for; matrix products, arithmetic and copies ran while one was open for 4% of the time, Pallas kernels for 0%

commit v1 on v0

v1 whole, which is shorter than its diff:
```python
import functools
import math

import jax
import jax.numpy as jnp
import numpy as np
from jax import lax
from jax.experimental import pallas as pl
from jax.experimental.pallas import tpu as pltpu
from jax.sharding import PartitionSpec as P

SUBPIX = 128
SPOT = 128
SUBX = 16
SLICES = 3
QUANT = 4
OVER = 2
PCOLS = 2048
DIRS = 4

CUTS = (0, 64, 128)
FINAL_COLS = 512
VMEM_LIMIT = 48 * 1024 * 1024


def tables():
    frequency = np.arange(SPOT, dtype=np.float64) - SPOT // 2
    position = np.arange(SUBPIX, dtype=np.float64) - (SUBPIX - 1) / 2.0
    angle = -2.0 * math.pi / (OVER * SUBPIX) * frequency[:, None] * position[None, :]
    factor = 1.0 / math.sqrt(SUBPIX)
    real_part = (np.cos(angle) * factor).astype(jnp.bfloat16)
    imag_part = (np.sin(angle) * factor).astype(jnp.bfloat16)
    right = np.block([[real_part.T, imag_part.T], [-imag_part.T, real_part.T]])
    return real_part.astype(np.float32), imag_part.astype(np.float32), right


def shifted(value, by):
    count = lax.axis_size("tile")
    return lax.ppermute(value, "tile", [(i, (i + by) % count) for i in range(count)])


def other_core(value):
    return lax.ppermute(value, "dir", [(0, 1), (1, 0), (2, 3), (3, 2)])


def other_chip(value):
    return lax.ppermute(value, "dir", [(0, 2), (1, 3), (2, 0), (3, 1)])


def term_kernel(first, rows, depths, index_ref, offsets_ref, *refs):
    blocks = refs[: len(depths)]
    outs = refs[len(depths) :]
    total = sum(depths)
    own = index_ref[0]
    wanted = (own, own ^ 2, own ^ 1, own ^ 3)
    parts = []
    for direction in wanted:
        steps = offsets_ref[direction, own, 0]
        start = steps >> 2
        frac = (steps & 3).astype(jnp.float32) * 0.25
        away = lax.broadcasted_iota(jnp.int32, (rows, total), 1) - lax.broadcasted_iota(
            jnp.int32, (rows, total), 0
        )
        parts.append(
            jnp.where(away == start, 1.0 - frac, jnp.where(away == start + 1, frac, 0.0))
        )
    select = jnp.concatenate(parts, 0).astype(jnp.bfloat16)
    down = None
    at = 0
    for block, depth in zip(blocks, depths):
        piece = jnp.dot(
            select[:, at : at + depth], block[...], preferred_element_type=jnp.float32
        )
        down = piece if down is None else down + piece
        at += depth
    for place, direction in enumerate(wanted):
        steps = offsets_ref[direction, own, 1]
        start = steps >> 2
        frac = (steps & 3).astype(jnp.float32) * 0.25
        rows_down = down[place * rows : (place + 1) * rows]
        near = pltpu.roll(rows_down, (PCOLS - start) & (PCOLS - 1), 1)
        far = pltpu.roll(near, PCOLS - 1, 1)
        term = ((1.0 - frac) * near + frac * far).astype(jnp.bfloat16)
        if place < 2:
            outs[place][...] = term
        else:
            outs[2][place - 2] = term


def terms(first, rows, index, offsets, blocks):
    depths = tuple(b.shape[0] for b in blocks)
    flat = jax.ShapeDtypeStruct((rows, PCOLS), jnp.bfloat16)
    whole = pl.BlockSpec(memory_space=pltpu.VMEM)
    return pl.pallas_call(
        functools.partial(term_kernel, first, rows, depths),
        out_shape=(flat, flat, jax.ShapeDtypeStruct((2, rows, PCOLS), jnp.bfloat16)),
        in_specs=[pl.BlockSpec(memory_space=pltpu.SMEM)] * 2 + [whole] * len(blocks),
        out_specs=(whole, whole, whole),
        compiler_params=pltpu.CompilerParams(vmem_limit_bytes=VMEM_LIMIT),
        name="terms",
    )(index, offsets, *blocks)


def series():
    points = 0.25 * (1.0 - np.cos(np.pi * (np.arange(4000) + 0.5) / 4000)) * 0.5
    basis = lambda count: np.stack([points**k for k in range(count)], 1)
    root = np.sqrt(points)
    sine = np.linalg.lstsq(basis(8), np.sin(2 * np.pi * root) / root, rcond=None)[0]
    cosine = np.linalg.lstsq(basis(8), np.cos(2 * np.pi * root), rcond=None)[0]
    return [float(c) for c in sine], [float(c) for c in cosine]


SINE, COSINE = series()


def horner(coefficients, square):
    value = jnp.full_like(square, coefficients[-1])
    for c in coefficients[-2::-1]:
        value = value * square + c
    return value


def final_kernel(chunks, scale_ref, valid_ref, left_ref, right_ref, column_ref, *refs):
    keeps, pairs, fars = refs[:chunks], refs[chunks : 2 * chunks], refs[2 * chunks : 3 * chunks]
    out_ref = refs[3 * chunks]
    cols = out_ref.shape[1]
    phase = jnp.concatenate(
        [
            (k[...].astype(jnp.float32) + p[0].astype(jnp.float32)) + f[...].astype(jnp.float32)
            for k, p, f in zip(keeps, pairs, fars)
        ],
        0,
    )
    turns = phase * (0.5 / math.pi)
    turns = turns - jnp.round(turns)
    square = turns * turns
    field = jnp.concatenate(
        [horner(COSINE, square), turns * horner(SINE, square)], 0
    ).astype(jnp.bfloat16)
    focal = jnp.dot(left_ref[...], field, preferred_element_type=jnp.float32)
    reals, imags = [], []
    for altitude in range(SLICES):
        real = focal[2 * SPOT * altitude : 2 * SPOT * altitude + SPOT]
        imag = focal[2 * SPOT * altitude + SPOT : 2 * SPOT * (altitude + 1)]
        cosine = column_ref[altitude : altitude + 1]
        sine = column_ref[SLICES + altitude : SLICES + altitude + 1]
        reals.append((real * cosine - imag * sine).astype(jnp.bfloat16))
        imags.append((real * sine + imag * cosine).astype(jnp.bfloat16))
    real = jnp.concatenate(reals, 0)
    imag = jnp.concatenate(imags, 0)
    for place in range(cols // SUBPIX):
        at = slice(place * SUBPIX, (place + 1) * SUBPIX)
        spot = jnp.dot(
            jnp.concatenate([real[:, at], imag[:, at]], 1),
            right_ref[...],
            preferred_element_type=jnp.float32,
        )
        power = spot * spot
        power = power[:, :SPOT] + power[:, SPOT:]
        total = None
        for altitude in range(SLICES):
            piece = scale_ref[altitude] * power[altitude * SPOT : (altitude + 1) * SPOT]
            total = piece if total is None else total + piece
        lit = valid_ref[0, pl.program_id(0) * (cols // SUBPIX) + place].astype(jnp.float32)
        out_ref[:, at] = (total * lit).astype(jnp.bfloat16)


def spots_of(scale, valid, left, right, column, keeps, pairs, fars):
    chunks = len(keeps)
    smem = pl.BlockSpec(memory_space=pltpu.SMEM)
    flat = [pl.BlockSpec((k.shape[0], FINAL_COLS), lambda i: (0, i)) for k in keeps]
    deep = [pl.BlockSpec((1, k.shape[0], FINAL_COLS), lambda i: (0, 0, i)) for k in keeps]
    return pl.pallas_call(
        functools.partial(final_kernel, chunks),
        grid=(PCOLS // FINAL_COLS,),
        out_shape=jax.ShapeDtypeStruct((SPOT, PCOLS), jnp.bfloat16),
        in_specs=[
            smem,
            smem,
            pl.BlockSpec(left.shape, lambda i: (0, 0)),
            pl.BlockSpec(right.shape, lambda i: (0, 0)),
            pl.BlockSpec((2 * SLICES, FINAL_COLS), lambda i: (0, i)),
        ]
        + flat
        + deep
        + flat,
        out_specs=pl.BlockSpec((SPOT, FINAL_COLS), lambda i: (0, i)),
        compiler_params=pltpu.CompilerParams(vmem_limit_bytes=VMEM_LIMIT),
        name="spots",
    )(scale, valid, left, right, column, *keeps, *pairs, *fars)


def shards(layers, offsets, subap_valid, defocus, weights):
    index = lax.axis_index("dir").astype(jnp.int32)[None]
    tile = lax.axis_index("tile")
    total_rows = lax.axis_size("tile") * SUBPIX
    block = layers[0]
    own = [block[a:b] for a, b in zip(CUTS, CUTS[1:])]
    once = [shifted(piece, -1) for piece in own]
    twice = [shifted(piece, -1) for piece in once]

    real_part, imag_part, right = tables()
    row = (
        (tile * SUBPIX + jnp.arange(SUBPIX, dtype=jnp.int32)).astype(jnp.float32)
        - (total_rows - 1) / 2.0
    ) / SUBPIX
    col = (jnp.arange(PCOLS, dtype=jnp.float32) - (PCOLS - 1) / 2.0) / SUBPIX
    row_angle = defocus[:, None] * (row * row)[None, :]
    col_angle = defocus[:, None] * (col * col)[None, :]
    row_cos, row_sin = jnp.cos(row_angle)[:, None], jnp.sin(row_angle)[:, None]
    left_real = real_part[None] * row_cos - imag_part[None] * row_sin
    left_imag = real_part[None] * row_sin + imag_part[None] * row_cos
    left = jnp.concatenate(
        [
            jnp.concatenate([left_real, -left_imag], 2),
            jnp.concatenate([left_imag, left_real], 2),
        ],
        1,
    )
    left = left.reshape(SLICES * 2 * SPOT, 2 * SUBPIX).astype(jnp.bfloat16)
    column = jnp.concatenate([jnp.cos(col_angle), jnp.sin(col_angle)], 0)
    scale = weights / jnp.sum(weights)

    keeps, pairs, fars = [], [], []
    for m, (a, b) in enumerate(zip(CUTS, CUTS[1:])):
        blocks = own[m:] + once + twice[: m + 1]
        keep, send, cross = terms(a, b - a, index, offsets, blocks)
        pair = other_core(cross)
        both = (send.astype(jnp.float32) + pair[1].astype(jnp.float32)).astype(jnp.bfloat16)
        keeps.append(keep)
        pairs.append(pair)
        fars.append(other_chip(both))
    spots = spots_of(scale, subap_valid, left, right, column, keeps, pairs, fars)
    return spots[None, None]


def solution(mesh):
    placed = (P("dir", "tile", None), P(), P("tile", None), P(), P())
    return jax.shard_map(
        shards, mesh=mesh, in_specs=placed, out_specs=P("dir", "tile", None, None), check_vma=False
    )
```

time: 237 us -> 76.4 us (0.32)
  waiting for transfers between devices: 143 us -> 15.3 us
  between operations: 34.9 us -> 0.21 us
  starting transfers between devices: 11.6 us -> 44.5 us
  other arithmetic: 31.4 us -> 1.95 us
  Pallas kernels: 0 us -> 11.6 us
  local copies, waits for them, and re-layouts: 11.9 us -> 2.53 us
  matrix products: 3.69 us -> 0 us
    ppermute x2 -> x8, waiting for transfers between devices: 100 us -> 15.3 us  [the longest x2 9.43 us: other_chip(): return lax.ppermute(value, 'dir', [(0, 2), (1, 3), (2, 0), (3, 1)])]
    all_gather x1 -> x0, waiting for transfers between devices: 42.3 us -> none  [shards(): stacked = lax.all_gather(layers, 'dir', axis=0, tiled=True)]
    ppermute x2 -> x8, starting transfers between devices: 11.6 us -> 44.5 us  [the longest x4 31.7 us: shifted(): lax.ppermute(value, 'tile', [(i, (i + by) % count) for i in range(count)])]
    another operation x3 -> x1, other arithmetic: 19.8 us -> 0.07 us
    pallas_call x0 -> x3, Pallas kernels: none -> 11.6 us  [the longest x2 6.38 us: terms(): pl.pallas_call(functools.partial(term_kernel, first, rows, depths), out_s...]
    add x4 -> x0, other arithmetic: 4.96 us -> none  [interpolate(): across = (1.0 - col_frac) * col_first + col_frac * col_second]
    slice x7 -> x1, local copies, waits for them, and re-layouts: 5.52 us -> 1.06 us  [shards(): own = [block[a:b] for a, b in zip(CUTS, CUTS[1:])]]
    dot_general x6 -> x0, matrix products: 3.69 us -> none  [the longest x3 2.38 us: spots_row(): jnp.dot(left_table, pupil_field, preferred_element_type=jnp.float32)]
  transfers between devices with their start and end apart: 3 -> 8, of which waited for: 3 -> 4; matrix products, arithmetic and copies ran while one was open for 4% -> 3% of each run, Pallas kernels for 0% -> 4%
where the time goes in v1:
time: 76.4 us; the launch traced here: 76 us
  starting transfers between devices  44.5 us (58%)
  waiting for transfers between devices  15.3 us (20%)
  Pallas kernels  11.6 us (15%)
  local copies, waits for them, and re-layouts  2.53 us (3%)
  other arithmetic  1.95 us (3%)
    ppermute x4, starting transfers between devices, shifted(): lax.ppermute(value, 'tile', [(i, (i + by) % count) for i in range(count)])  31.7 us
    ppermute x2, waiting for transfers between devices, other_chip(): return lax.ppermute(value, 'dir', [(0, 2), (1, 3), (2, 0), (3, 1)])  9.43 us
    ppermute x2, starting transfers between devices, other_chip(): return lax.ppermute(value, 'dir', [(0, 2), (1, 3), (2, 0), (3, 1)])  6.79 us
    pallas_call x2, Pallas kernels, terms(): pl.pallas_call(functools.partial(term_kernel, first, rows, depths), out_s...  6.38 us
    ppermute x2, starting transfers between devices, other_core(): return lax.ppermute(value, 'dir', [(0, 1), (1, 0), (2, 3), (3, 2)])  5.96 us
    ppermute x4, waiting for transfers between devices, shifted(): lax.ppermute(value, 'tile', [(i, (i + by) % count) for i in range(count)])  5.87 us
    pallas_call x1, Pallas kernels, spots_of(): pl.pallas_call(functools.partial(final_kernel, chunks), grid=(PCOLS // FI...  5.22 us
  transfers between devices with their start and end apart: 8, of which 4 were waited for; matrix products, arithmetic and copies ran while one was open for 3% of the time, Pallas kernels for 4%

profile of v1, /device:TPU:1, one launch (start us, length us, event | category | flops | bytes accessed | tf_op | source)
XLA Modules:
  0.0 76.0 jit_solution(8702039555708655241)
XLA Ops:
  0.0 1.1 %slice_bitcast_fusion.2 = (bf16[64,2048]{1,0:T(8,128)(2,1)S(1)}, bf16[64,2048]{1,0:T(8,128)(2,1)S(1)}) fusion(bf16[1,128,2048]{2,1,0:T(8,128)(2,1)} %param.10), kind=kLoop, calls=%fused_computation.7 | loop fusion | bytes 1048576 | tf_op jit(solution)/shard_map/slice | solution.py:198
  1.1 15.2 %collective-permute-start = (bf16[64,2048]{1,0:T(8,128)(2,1)S(1)}, bf16[64,2048]{1,0:T(8,128)(2,1)S(1)}, u32[]{:S(2)}, u32[]{:S(2)}) collective-permute-start(bf16[64,2048]{1,0:T(8,128)(2,1)S(1)} %get-tuple-element.18.refs_0_), channel_id=1, source_target_pairs={{0,508},{4,0},{8,4},{12,8},{16,12},{20,16},{24,20},{28,24},{32,28}... | collective-permute-start | bytes 786440 | tf_op jit(solution)/shard_map/ppermute | solution.py:39
  16.2 0.0 copy-start.5
  16.2 2.6 %collective-permute-start.1 = (bf16[64,2048]{1,0:T(8,128)(2,1)S(1)}, bf16[64,2048]{1,0:T(8,128)(2,1)S(1)}, u32[]{:S(2)}, u32[]{:S(2)}) collective-permute-start(bf16[64,2048]{1,0:T(8,128)(2,1)S(1)} %get-tuple-element.17.refs_1_.refs_0_), channel_id=1, source_target_pairs={{0,508},{4,0},{8,4},{12,8},{16,12},{20,16},{24,20},{28,24},{32,28}... | collective-permute-start | bytes 786440 | tf_op jit(solution)/shard_map/ppermute | solution.py:39
  18.9 2.3 %collective-permute-done.refs_2_.refs_1_ = bf16[64,2048]{1,0:T(8,128)(2,1)S(1)} collective-permute-done((bf16[64,2048]{1,0:T(8,128)(2,1)S(1)}, bf16[64,2048]{1,0:T(8,128)(2,1)S(1)}, u32[]{:S(2)}, u32[]{:S(2)}) %collective-permute-start) | collective-permute-done | bytes 262176 | tf_op jit(solution)/shard_map/ppermute | solution.py:39
  21.2 8.3 %collective-permute-start.2 = (bf16[64,2048]{1,0:T(8,128)(2,1)S(1)}, bf16[64,2048]{1,0:T(8,128)(2,1)S(1)}, u32[]{:S(2)}, u32[]{:S(2)}) collective-permute-start(bf16[64,2048]{1,0:T(8,128)(2,1)S(1)} %collective-permute-done.refs_2_.refs_1_), channel_id=1, source_target_pairs={{0,508},{4,0},{8,4},{12,8},{16,12},{20,16},{24,20},{28,24},{32,28}... | collective-permute-start | bytes 786440 | tf_op jit(solution)/shard_map/ppermute | solution.py:39
  29.5 0.0 collective-permute-done.1.refs_3_.refs_2_
  29.5 5.6 %collective-permute-start.3 = (bf16[64,2048]{1,0:T(8,128)(2,1)S(1)}, bf16[64,2048]{1,0:T(8,128)(2,1)S(1)}, u32[]{:S(2)}, u32[]{:S(2)}) collective-permute-start(bf16[64,2048]{1,0:T(8,128)(2,1)S(1)} %collective-permute-done.1.refs_3_.refs_2_), channel_id=1, source_target_pairs={{0,508},{4,0},{8,4},{12,8},{16,12},{20,16},{24,20},{28,24},{32,28}... | collective-permute-start | bytes 786440 | tf_op jit(solution)/shard_map/ppermute | solution.py:39
  35.1 0.0 copy-done.5
  35.1 0.3 multiply_cosine_fusion
  35.4 0.0 copy-start.4
  35.5 0.7 copy-done.4
  36.1 0.1 copy.11.offsets_ref
  36.3 0.0 collective-permute-done.2.refs_4_.refs_3_
  36.3 3.6 %collective-permute-done.3.refs_4_ = bf16[64,2048]{1,0:T(8,128)(2,1)S(1)} collective-permute-done((bf16[64,2048]{1,0:T(8,128)(2,1)S(1)}, bf16[64,2048]{1,0:T(8,128)(2,1)S(1)}, u32[]{:S(2)}, u32[]{:S(2)}) %collective-permute-start.3) | collective-permute-done | bytes 262176 | tf_op jit(solution)/shard_map/ppermute | solution.py:39
  39.8 0.0 copy-start.2
  39.9 0.0 copy-start.3
  39.9 3.2 %terms.3 = (bf16[64,2048]{1,0:T(8,128)(2,1)S(1)}, bf16[64,2048]{1,0:T(8,128)(2,1)S(1)}, bf16[2,64,2048]{2,1,0:T(8,128)(2,1)S(1)}) custom-call(s32[1]{0:T(128)} %bitcast.1.index_ref, s32[4,4,2]{2,1,0:T(4,128)S(1)} %copy.11.offsets_ref, bf16[64,2048]{1,0:T(8,128)(2,1)S(1)} %get-tuple-element.17.refs_1_.refs_0_, ...), custom_call_target="tpu_custom_call" | custom-call | tf_op jit(solution)/shard_map/terms/pallas_call | solution.py:94
  43.0 0.0 copy-start.6
  43.1 4.0 %collective-permute-start.5 = (bf16[2,64,2048]{2,1,0:T(8,128)(2,1)S(1)}, bf16[2,64,2048]{2,1,0:T(8,128)(2,1)S(1)}, u32[]{:S(2)}, u32[]{:S(2)}) collective-permute-start(bf16[2,64,2048]{2,1,0:T(8,128)(2,1)S(1)} %get-tuple-element.14), channel_id=1, source_target_pairs={{0,1},{1,0},{2,3},{3,2},{4,5},{5,4},{6,7},{7,6},{8,9},{9,8},{10,11... | collective-permute-start | bytes 1572872 | tf_op jit(solution)/shard_map/ppermute | solution.py:43
  47.1 0.1 multiply_cosine_fusion.1
  47.2 0.0 copy-done.6
  47.2 0.6 reduce_sum.9
  47.8 0.0 copy-done.2
  47.8 0.0 copy-done.3
  47.8 0.1 negate_convert_fusion
  47.9 3.2 %terms.2 = (bf16[64,2048]{1,0:T(8,128)(2,1)S(1)}, bf16[64,2048]{1,0:T(8,128)(2,1)S(1)}, bf16[2,64,2048]{2,1,0:T(8,128)(2,1)S(1)}) custom-call(s32[1]{0:T(128)} %bitcast.1.index_ref, s32[4,4,2]{2,1,0:T(4,128)S(1)} %copy.11.offsets_ref, bf16[64,2048]{1,0:T(8,128)(2,1)S(1)} %get-tuple-element.18.refs_0_, ...), custom_call_target="tpu_custom_call" | custom-call | tf_op jit(solution)/shard_map/terms/pallas_call | solution.py:94
  51.1 1.9 %collective-permute-start.4 = (bf16[2,64,2048]{2,1,0:T(8,128)(2,1)S(1)}, bf16[2,64,2048]{2,1,0:T(8,128)(2,1)S(1)}, u32[]{:S(2)}, u32[]{:S(2)}) collective-permute-start(bf16[2,64,2048]{2,1,0:T(8,128)(2,1)S(1)} %get-tuple-element.13), channel_id=1, source_target_pairs={{0,1},{1,0},{2,3},{3,2},{4,5},{5,4},{6,7},{7,6},{8,9},{9,8},{10,11... | collective-permute-start | bytes 1572872 | tf_op jit(solution)/shard_map/ppermute | solution.py:43
  53.0 0.7 broadcast_divide_fusion.scale_ref
  53.7 0.0 collective-permute-done.5.refs_3_
  53.7 0.1 fusion
  53.8 4.5 %collective-permute-start.7 = (bf16[64,2048]{1,0:T(8,128)(2,1)S(1)}, bf16[64,2048]{1,0:T(8,128)(2,1)S(1)}, u32[]{:S(2)}, u32[]{:S(2)}) collective-permute-start(bf16[64,2048]{1,0:T(8,128)(2,1)S(1)} %fusion), channel_id=1, source_target_pairs={{0,2},{1,3},{2,0},{3,1},{4,6},{5,7},{6,4},{7,5},{8,10},{9,11},{10,... | collective-permute-start | bytes 786440 | tf_op jit(solution)/shard_map/ppermute | solution.py:47
  58.3 0.0 collective-permute-done.4.refs_2_
  58.3 0.1 fusion.1
  58.4 2.3 %collective-permute-start.6 = (bf16[64,2048]{1,0:T(8,128)(2,1)S(1)}, bf16[64,2048]{1,0:T(8,128)(2,1)S(1)}, u32[]{:S(2)}, u32[]{:S(2)}) collective-permute-start(bf16[64,2048]{1,0:T(8,128)(2,1)S(1)} %fusion.1), channel_id=1, source_target_pairs={{0,2},{1,3},{2,0},{3,1},{4,6},{5,7},{6,4},{7,5},{8,10},{9,11},{10,... | collective-permute-start | bytes 786440 | tf_op jit(solution)/shard_map/ppermute | solution.py:47
  60.7 0.0 copy-start
  60.7 3.8 %collective-permute-done.7.refs_5_ = bf16[64,2048]{1,0:T(8,128)(2,1)S(1)} collective-permute-done((bf16[64,2048]{1,0:T(8,128)(2,1)S(1)}, bf16[64,2048]{1,0:T(8,128)(2,1)S(1)}, u32[]{:S(2)}, u32[]{:S(2)}) %collective-permute-start.7) | collective-permute-done | bytes 262176 | tf_op jit(solution)/shard_map/ppermute | solution.py:47
  64.6 5.6 %collective-permute-done.6.refs_4_ = bf16[64,2048]{1,0:T(8,128)(2,1)S(1)} collective-permute-done((bf16[64,2048]{1,0:T(8,128)(2,1)S(1)}, bf16[64,2048]{1,0:T(8,128)(2,1)S(1)}, u32[]{:S(2)}, u32[]{:S(2)}) %collective-permute-start.6) | collective-permute-done | bytes 262176 | tf_op jit(solution)/shard_map/ppermute | solution.py:47
  70.2 0.0 copy-start.1
  70.2 0.0 copy-done
  70.2 0.7 copy-done.1
  70.8 5.2 %spots.1 = bf16[128,2048]{1,0:T(8,128)(2,1)} custom-call(f32[3]{0:T(128)S(1)} %broadcast_divide_fusion.scale_ref, s32[1,16]{1,0:T(1,128)S(1)} %copy-done.1, bf16[768,256]{1,0:T(8,128)(2,1)S(1)} %bitcast.17, bf16[256,256]{1,0:T(8,128)(2,1)S(1)} %copy-done, f32[6,2048]{1,0:T(8,128)S(1)} %pad_maximum_fusion.column_ref, ...), custom_call_target="tpu_custom_call" | custom-call | tf_op jit(solution)/shard_map/spots/pallas_call | solution.py:173
  (4 shorter events, 0.1 us)
Async XLA Ops:
  1.1 20.1 %collective-permute-start = (bf16[64,2048]{1,0:T(8,128)(2,1)S(1)}, bf16[64,2048]{1,0:T(8,128)(2,1)S(1)}, u32[]{:S(2)}, u32[]{:S(2)}) collective-permute-start(bf16[64,2048]{1,0:T(8,128)(2,1)S(1)} %get-tuple-element.18.refs_0_), channel_id=1, source_target_pairs={{0,508},{4,0},{8,4},{12,8},{16,12},{20,16},{24,20},{28,24},{32,28}... | collective-permute-start | bytes 786440 | tf_op jit(solution)/shard_map/ppermute | solution.py:39
  16.2 18.9 %copy-start.5 = (f32[3]{0:T(128)S(1)}, f32[3]{0:T(128)}, u32[]{:S(2)}) copy-start(f32[3]{0:T(128)} %param.13) | copy-start | bytes 40
  16.2 13.3 %collective-permute-start.1 = (bf16[64,2048]{1,0:T(8,128)(2,1)S(1)}, bf16[64,2048]{1,0:T(8,128)(2,1)S(1)}, u32[]{:S(2)}, u32[]{:S(2)}) collective-permute-start(bf16[64,2048]{1,0:T(8,128)(2,1)S(1)} %get-tuple-element.17.refs_1_.refs_0_), channel_id=1, source_target_pairs={{0,508},{4,0},{8,4},{12,8},{16,12},{20,16},{24,20},{28,24},{32,28}... | collective-permute-start | bytes 786440 | tf_op jit(solution)/shard_map/ppermute | solution.py:39
  21.2 15.1 %collective-permute-start.2 = (bf16[64,2048]{1,0:T(8,128)(2,1)S(1)}, bf16[64,2048]{1,0:T(8,128)(2,1)S(1)}, u32[]{:S(2)}, u32[]{:S(2)}) collective-permute-start(bf16[64,2048]{1,0:T(8,128)(2,1)S(1)} %collective-permute-done.refs_2_.refs_1_), channel_id=1, source_target_pairs={{0,508},{4,0},{8,4},{12,8},{16,12},{20,16},{24,20},{28,24},{32,28}... | collective-permute-start | bytes 786440 | tf_op jit(solution)/shard_map/ppermute | solution.py:39
  29.5 10.3 %collective-permute-start.3 = (bf16[64,2048]{1,0:T(8,128)(2,1)S(1)}, bf16[64,2048]{1,0:T(8,128)(2,1)S(1)}, u32[]{:S(2)}, u32[]{:S(2)}) collective-permute-start(bf16[64,2048]{1,0:T(8,128)(2,1)S(1)} %collective-permute-done.1.refs_3_.refs_2_), channel_id=1, source_target_pairs={{0,508},{4,0},{8,4},{12,8},{16,12},{20,16},{24,20},{28,24},{32,28}... | collective-permute-start | bytes 786440 | tf_op jit(solution)/shard_map/ppermute | solution.py:39
  35.4 0.7 copy-start.4
  39.8 8.0 %copy-start.2 = (f32[128,128]{1,0:T(8,128)S(1)}, f32[128,128]{1,0:T(8,128)}, u32[]{:S(2)}) copy-start(f32[128,128]{1,0:T(8,128)} %constant.35) | copy-start | bytes 196612
  39.9 8.0 %copy-start.3 = (f32[128,128]{1,0:T(8,128)S(1)}, f32[128,128]{1,0:T(8,128)}, u32[]{:S(2)}) copy-start(f32[128,128]{1,0:T(8,128)} %constant.36) | copy-start | bytes 196612
  43.0 4.2 %copy-start.6 = (f32[3]{0:T(128)S(1)}, f32[3]{0:T(128)}, u32[]{:S(2)}) copy-start(f32[3]{0:T(128)} %param.14) | copy-start | bytes 40
  43.1 10.6 %collective-permute-start.5 = (bf16[2,64,2048]{2,1,0:T(8,128)(2,1)S(1)}, bf16[2,64,2048]{2,1,0:T(8,128)(2,1)S(1)}, u32[]{:S(2)}, u32[]{:S(2)}) collective-permute-start(bf16[2,64,2048]{2,1,0:T(8,128)(2,1)S(1)} %get-tuple-element.14), channel_id=1, source_target_pairs={{0,1},{1,0},{2,3},{3,2},{4,5},{5,4},{6,7},{7,6},{8,9},{9,8},{10,11... | collective-permute-start | bytes 1572872 | tf_op jit(solution)/shard_map/ppermute | solution.py:43
  51.1 7.2 %collective-permute-start.4 = (bf16[2,64,2048]{2,1,0:T(8,128)(2,1)S(1)}, bf16[2,64,2048]{2,1,0:T(8,128)(2,1)S(1)}, u32[]{:S(2)}, u32[]{:S(2)}) collective-permute-start(bf16[2,64,2048]{2,1,0:T(8,128)(2,1)S(1)} %get-tuple-element.13), channel_id=1, source_target_pairs={{0,1},{1,0},{2,3},{3,2},{4,5},{5,4},{6,7},{7,6},{8,9},{9,8},{10,11... | collective-permute-start | bytes 1572872 | tf_op jit(solution)/shard_map/ppermute | solution.py:43
  53.8 10.8 %collective-permute-start.7 = (bf16[64,2048]{1,0:T(8,128)(2,1)S(1)}, bf16[64,2048]{1,0:T(8,128)(2,1)S(1)}, u32[]{:S(2)}, u32[]{:S(2)}) collective-permute-start(bf16[64,2048]{1,0:T(8,128)(2,1)S(1)} %fusion), channel_id=1, source_target_pairs={{0,2},{1,3},{2,0},{3,1},{4,6},{5,7},{6,4},{7,5},{8,10},{9,11},{10,... | collective-permute-start | bytes 786440 | tf_op jit(solution)/shard_map/ppermute | solution.py:47
  58.4 11.8 %collective-permute-start.6 = (bf16[64,2048]{1,0:T(8,128)(2,1)S(1)}, bf16[64,2048]{1,0:T(8,128)(2,1)S(1)}, u32[]{:S(2)}, u32[]{:S(2)}) collective-permute-start(bf16[64,2048]{1,0:T(8,128)(2,1)S(1)} %fusion.1), channel_id=1, source_target_pairs={{0,2},{1,3},{2,0},{3,1},{4,6},{5,7},{6,4},{7,5},{8,10},{9,11},{10,... | collective-permute-start | bytes 786440 | tf_op jit(solution)/shard_map/ppermute | solution.py:47
  60.7 9.5 %copy-start = (bf16[256,256]{1,0:T(8,128)(2,1)S(1)}, bf16[256,256]{1,0:T(8,128)(2,1)}, u32[]{:S(2)}) copy-start(bf16[256,256]{1,0:T(8,128)(2,1)} %constant.32.clone.right_ref) | copy-start | bytes 393220
  70.2 0.7 copy-start.1

commit v2 on v1

--- a/solution.py
+++ b/solution.py
@@ -20,6 +20,8 @@
 
 CUTS = (0, 64, 128)
 FINAL_COLS = 512
+LANES = 128
+GROUP = 256
 VMEM_LIMIT = 48 * 1024 * 1024
 
 
@@ -65,26 +67,59 @@
             jnp.where(away == start, 1.0 - frac, jnp.where(away == start + 1, frac, 0.0))
         )
     select = jnp.concatenate(parts, 0).astype(jnp.bfloat16)
-    down = None
-    at = 0
-    for block, depth in zip(blocks, depths):
-        piece = jnp.dot(
-            select[:, at : at + depth], block[...], preferred_element_type=jnp.float32
-        )
-        down = piece if down is None else down + piece
-        at += depth
+    lane = lax.broadcasted_iota(jnp.int32, (rows, LANES), 1)
+    moves = []
     for place, direction in enumerate(wanted):
         steps = offsets_ref[direction, own, 1]
         start = steps >> 2
         frac = (steps & 3).astype(jnp.float32) * 0.25
-        rows_down = down[place * rows : (place + 1) * rows]
-        near = pltpu.roll(rows_down, (PCOLS - start) & (PCOLS - 1), 1)
-        far = pltpu.roll(near, PCOLS - 1, 1)
-        term = ((1.0 - frac) * near + frac * far).astype(jnp.bfloat16)
-        if place < 2:
-            outs[place][...] = term
-        else:
-            outs[2][place - 2] = term
+        within = start & (LANES - 1)
+        moves.append((start >> 7, within, (LANES - within) & (LANES - 1), frac))
+
+    def columns(at):
+        window = jnp.concatenate([block[:, at : at + GROUP] for block in blocks], 0)
+        down = jnp.dot(select, window, preferred_element_type=jnp.float32)
+        return [down[:, k : k + LANES] for k in range(0, GROUP, LANES)]
+
+    wide = lax.broadcasted_iota(jnp.int32, (DIRS * rows, LANES), 1)
+
+    def finish(place, k, here, after):
+        skip, within = moves[place][:2]
+        term = jnp.where(lane < LANES - within, here, after).astype(jnp.bfloat16)
+        to = pl.ds(pl.multiple_of(((k - skip) & (PCOLS // LANES - 1)) * LANES, LANES), LANES)
+        outs[place][:, to] = term
+
+    def turned(value, ahead):
+        out = []
+        for place in range(DIRS):
+            at = slice(place * rows, (place + 1) * rows)
+            _, _, turn, frac = moves[place]
+            out.append(pltpu.roll((1.0 - frac) * value[at] + frac * ahead[at], turn, 1))
+        return out
+
+    def shift(value):
+        return pltpu.roll(value, LANES - 1, 1)
+
+    count = PCOLS // LANES
+    values, shifts, turns = {}, {}, {}
+
+    def get(k):
+        if k not in values:
+            k -= k % (GROUP // LANES)
+            for n, value in enumerate(columns(k * LANES)):
+                values[k + n] = value
+                shifts[k + n] = shift(value)
+
+    get(0)
+    for k in range(count):
+        get((k + 1) % count)
+        ahead = jnp.where(wide < LANES - 1, shifts[k], shifts[(k + 1) % count])
+        turns[k] = turned(values[k], ahead)
+        if k:
+            for place in range(DIRS):
+                finish(place, k - 1, turns[k - 1][place], turns[k][place])
+    for place in range(DIRS):
+        finish(place, count - 1, turns[count - 1][place], turns[0][place])
 
 
 def terms(first, rows, index, offsets, blocks):
@@ -93,10 +128,11 @@
     whole = pl.BlockSpec(memory_space=pltpu.VMEM)
     return pl.pallas_call(
         functools.partial(term_kernel, first, rows, depths),
-        out_shape=(flat, flat, jax.ShapeDtypeStruct((2, rows, PCOLS), jnp.bfloat16)),
+        out_shape=(flat,) * DIRS,
         in_specs=[pl.BlockSpec(memory_space=pltpu.SMEM)] * 2 + [whole] * len(blocks),
-        out_specs=(whole, whole, whole),
+        out_specs=(whole,) * DIRS,
         compiler_params=pltpu.CompilerParams(vmem_limit_bytes=VMEM_LIMIT),
+        cost_estimate=pl.CostEstimate(flops=1024, bytes_accessed=1024, transcendentals=0),
         name="terms",
     )(index, offsets, *blocks)
 
@@ -120,13 +156,13 @@
     return value
 
 
-def final_kernel(chunks, scale_ref, valid_ref, left_ref, right_ref, column_ref, *refs):
+def final_kernel(chunks, left_ref, right_ref, column_ref, *refs):
     keeps, pairs, fars = refs[:chunks], refs[chunks : 2 * chunks], refs[2 * chunks : 3 * chunks]
     out_ref = refs[3 * chunks]
     cols = out_ref.shape[1]
     phase = jnp.concatenate(
         [
-            (k[...].astype(jnp.float32) + p[0].astype(jnp.float32)) + f[...].astype(jnp.float32)
+            (k[...].astype(jnp.float32) + p[...].astype(jnp.float32)) + f[...].astype(jnp.float32)
             for k, p, f in zip(keeps, pairs, fars)
         ],
         0,
@@ -159,35 +195,29 @@
         power = power[:, :SPOT] + power[:, SPOT:]
         total = None
         for altitude in range(SLICES):
-            piece = scale_ref[altitude] * power[altitude * SPOT : (altitude + 1) * SPOT]
+            piece = power[altitude * SPOT : (altitude + 1) * SPOT]
             total = piece if total is None else total + piece
-        lit = valid_ref[0, pl.program_id(0) * (cols // SUBPIX) + place].astype(jnp.float32)
+        lit = column_ref[2 * SLICES : 2 * SLICES + 1, at]
         out_ref[:, at] = (total * lit).astype(jnp.bfloat16)
 
 
-def spots_of(scale, valid, left, right, column, keeps, pairs, fars):
+def spots_of(left, right, column, keeps, pairs, fars):
     chunks = len(keeps)
-    smem = pl.BlockSpec(memory_space=pltpu.SMEM)
     flat = [pl.BlockSpec((k.shape[0], FINAL_COLS), lambda i: (0, i)) for k in keeps]
-    deep = [pl.BlockSpec((1, k.shape[0], FINAL_COLS), lambda i: (0, 0, i)) for k in keeps]
     return pl.pallas_call(
         functools.partial(final_kernel, chunks),
         grid=(PCOLS // FINAL_COLS,),
         out_shape=jax.ShapeDtypeStruct((SPOT, PCOLS), jnp.bfloat16),
         in_specs=[
-            smem,
-            smem,
             pl.BlockSpec(left.shape, lambda i: (0, 0)),
             pl.BlockSpec(right.shape, lambda i: (0, 0)),
-            pl.BlockSpec((2 * SLICES, FINAL_COLS), lambda i: (0, i)),
+            pl.BlockSpec((2 * SLICES + 1, FINAL_COLS), lambda i: (0, i)),
         ]
-        + flat
-        + deep
-        + flat,
+        + flat * 3,
         out_specs=pl.BlockSpec((SPOT, FINAL_COLS), lambda i: (0, i)),
         compiler_params=pltpu.CompilerParams(vmem_limit_bytes=VMEM_LIMIT),
         name="spots",
-    )(scale, valid, left, right, column, *keeps, *pairs, *fars)
+    )(left, right, column, *keeps, *pairs, *fars)
 
 
 def shards(layers, offsets, subap_valid, defocus, weights):
@@ -197,7 +227,6 @@
     block = layers[0]
     own = [block[a:b] for a, b in zip(CUTS, CUTS[1:])]
     once = [shifted(piece, -1) for piece in own]
-    twice = [shifted(piece, -1) for piece in once]
 
     real_part, imag_part, right = tables()
     row = (
@@ -218,19 +247,33 @@
         1,
     )
     left = left.reshape(SLICES * 2 * SPOT, 2 * SUBPIX).astype(jnp.bfloat16)
-    column = jnp.concatenate([jnp.cos(col_angle), jnp.sin(col_angle)], 0)
-    scale = weights / jnp.sum(weights)
-
-    keeps, pairs, fars = [], [], []
-    for m, (a, b) in enumerate(zip(CUTS, CUTS[1:])):
-        blocks = own[m:] + once + twice[: m + 1]
-        keep, send, cross = terms(a, b - a, index, offsets, blocks)
-        pair = other_core(cross)
-        both = (send.astype(jnp.float32) + pair[1].astype(jnp.float32)).astype(jnp.bfloat16)
-        keeps.append(keep)
-        pairs.append(pair)
-        fars.append(other_chip(both))
-    spots = spots_of(scale, subap_valid, left, right, column, keeps, pairs, fars)
+    share = jnp.sqrt(weights / jnp.sum(weights))[:, None]
+    lit = jnp.repeat(subap_valid.astype(jnp.float32), SUBPIX, axis=1)
+    column = jnp.concatenate([jnp.cos(col_angle) * share, jnp.sin(col_angle) * share, lit], 0)
+
+    once[0], offsets, left, column = lax.optimization_barrier((once[0], offsets, left, column))
+    twice = [shifted(piece, -1) for piece in once]
+
+    blocks = own + once + twice[:1]
+    keep, send, cross, cross_send = terms(0, CUTS[1], index, offsets, blocks)
+    joined = other_core(cross_send)
+    joined, twice[1] = lax.optimization_barrier((joined, twice[1]))
+    both = (send.astype(jnp.float32) + joined.astype(jnp.float32)).astype(jnp.bfloat16)
+    both, twice[1] = lax.optimization_barrier((both, twice[1]))
+    keeps, crosses, fars = [keep], [cross], [other_chip(both)]
+
+    blocks = own[1:] + once + twice
+    keep, send, cross, cross_send = terms(CUTS[1], CUTS[2] - CUTS[1], index, offsets, blocks)
+    joined = other_core(cross_send)
+    send, fars[0] = lax.optimization_barrier((send, fars[0]))
+    both = (send.astype(jnp.float32) + joined.astype(jnp.float32)).astype(jnp.bfloat16)
+    crosses.append(cross)
+    keeps.append(keep)
+    fars.append(other_chip(both))
+    crosses[0], crosses[1], both = lax.optimization_barrier((crosses[0], crosses[1], both))
+    pairs = [other_core(cross) for cross in crosses]
+    fars[1], column = lax.optimization_barrier((fars[1], column))
+    spots = spots_of(left, right, column, keeps, pairs, fars)
     return spots[None, None]
 
 

time: 76.4 us -> 69.7 us (0.912)
  waiting for transfers between devices: 15.3 us -> 4.75 us
  starting transfers between devices: 44.5 us -> 52.4 us
  Pallas kernels: 11.6 us -> 8.51 us
  local copies, waits for them, and re-layouts: 2.53 us -> 1.33 us
    ppermute x2, waiting for transfers between devices: 9.43 us -> 1.97 us  [other_chip(): return lax.ppermute(value, 'dir', [(0, 2), (1, 3), (2, 0), (3, 1)])]
    ppermute x2 -> x4, starting transfers between devices: 5.96 us -> 11.6 us  [other_core(): return lax.ppermute(value, 'dir', [(0, 1), (1, 0), (2, 3), (3, 2)])]
    ppermute x4, waiting for transfers between devices: 5.87 us -> 0.28 us  [shifted(): lax.ppermute(value, 'tile', [(i, (i + by) % count) for i in range(count)])]
    ppermute x2 -> x4, waiting for transfers between devices: 0.01 us -> 2.5 us  [other_core(): return lax.ppermute(value, 'dir', [(0, 1), (1, 0), (2, 3), (3, 2)])]
    pallas_call x2, Pallas kernels: 6.38 us -> 3.91 us  [terms(): pl.pallas_call(functools.partial(term_kernel, first, rows, depths), out_s...]
    ppermute x2, starting transfers between devices: 6.79 us -> 9.07 us  [other_chip(): return lax.ppermute(value, 'dir', [(0, 2), (1, 3), (2, 0), (3, 1)])]
    unnamed x15 -> x14, local copies, waits for them, and re-layouts: 1.47 us -> 0.03 us
  transfers between devices with their start and end apart: 8 -> 10, of which waited for: 4 -> 5; matrix products, arithmetic and copies ran while one was open for 3% -> 3% of each run, Pallas kernels for 4% -> 6%
where the time goes in v2:
time: 69.7 us; the launch traced here: 69.2 us
  starting transfers between devices  52.4 us (75%)
  Pallas kernels  8.51 us (12%)
  waiting for transfers between devices  4.75 us (7%)
  other arithmetic  1.97 us (3%)
  local copies, waits for them, and re-layouts  1.33 us (2%)
    ppermute x4, starting transfers between devices, shifted(): lax.ppermute(value, 'tile', [(i, (i + by) % count) for i in range(count)])  31.7 us
    ppermute x4, starting transfers between devices, other_core(): return lax.ppermute(value, 'dir', [(0, 1), (1, 0), (2, 3), (3, 2)])  11.6 us
    ppermute x2, starting transfers between devices, other_chip(): return lax.ppermute(value, 'dir', [(0, 2), (1, 3), (2, 0), (3, 1)])  9.07 us
    pallas_call x1, Pallas kernels, spots_of(): pl.pallas_call(functools.partial(final_kernel, chunks), grid=(PCOLS // FI...  4.6 us
    pallas_call x2, Pallas kernels, terms(): pl.pallas_call(functools.partial(term_kernel, first, rows, depths), out_s...  3.91 us
    ppermute x4, waiting for transfers between devices, other_core(): return lax.ppermute(value, 'dir', [(0, 1), (1, 0), (2, 3), (3, 2)])  2.5 us
    ppermute x2, waiting for transfers between devices, other_chip(): return lax.ppermute(value, 'dir', [(0, 2), (1, 3), (2, 0), (3, 1)])  1.97 us
  transfers between devices with their start and end apart: 10, of which 5 were waited for; matrix products, arithmetic and copies ran while one was open for 3% of the time, Pallas kernels for 6%

profile of v2, /device:TPU:1, one launch (start us, length us, event | category | flops | bytes accessed | tf_op | source)
XLA Modules:
  0.0 69.2 jit_solution(17071968682271306648)
XLA Ops:
  0.0 0.0 copy-start.5
  0.0 0.0 copy-start.6
  0.0 0.0 copy-start.4
  0.0 0.0 copy-start.2
  0.0 1.1 %slice_bitcast_fusion = (bf16[64,2048]{1,0:T(8,128)(2,1)S(1)}, bf16[64,2048]{1,0:T(8,128)(2,1)S(1)}) fusion(bf16[1,128,2048]{2,1,0:T(8,128)(2,1)} %param.10), kind=kLoop, calls=%fused_computation.3 | loop fusion | bytes 1048576 | tf_op jit(solution)/shard_map/slice | solution.py:228
  1.1 0.0 copy-start.1
  1.2 15.3 %collective-permute-start = (bf16[64,2048]{1,0:T(8,128)(2,1)S(1)}, bf16[64,2048]{1,0:T(8,128)(2,1)S(1)}, u32[]{:S(2)}, u32[]{:S(2)}) collective-permute-start(bf16[64,2048]{1,0:T(8,128)(2,1)S(1)} %get-tuple-element.50.refs_0_), channel_id=1, source_target_pairs={{0,508},{4,0},{8,4},{12,8},{16,12},{20,16},{24,20},{28,24},{32,28}... | collective-permute-start | bytes 786440 | tf_op jit(solution)/shard_map/ppermute | solution.py:41
  16.5 2.6 %collective-permute-start.1 = (bf16[64,2048]{1,0:T(8,128)(2,1)S(1)}, bf16[64,2048]{1,0:T(8,128)(2,1)S(1)}, u32[]{:S(2)}, u32[]{:S(2)}) collective-permute-start(bf16[64,2048]{1,0:T(8,128)(2,1)S(1)} %get-tuple-element.49.refs_1_.refs_0_), channel_id=1, source_target_pairs={{0,508},{4,0},{8,4},{12,8},{16,12},{20,16},{24,20},{28,24},{32,28}... | collective-permute-start | bytes 786440 | tf_op jit(solution)/shard_map/ppermute | solution.py:41
  19.1 0.0 copy-done.5
  19.1 0.6 reduce_sum.9
  19.7 0.7 divide_sqrt_fusion
  20.4 0.0 copy-done.6
  20.4 0.0 copy-done.4
  20.4 0.1 multiply_cosine_fusion.1
  20.5 0.3 fusion.1
  20.9 0.0 copy-done.2
  20.9 0.0 copy-done.1
  20.9 0.1 negate_convert_fusion
  21.0 0.1 broadcast_in_dim.8
  21.1 0.0 copy-start.3
  21.1 0.3 collective-permute-done.refs_2_.refs_1_
  21.4 8.3 %collective-permute-start.2 = (bf16[64,2048]{1,0:T(8,128)(2,1)S(1)}, bf16[64,2048]{1,0:T(8,128)(2,1)S(1)}, u32[]{:S(2)}, u32[]{:S(2)}) collective-permute-start(bf16[64,2048]{1,0:T(8,128)(2,1)S(1)} %collective-permute-done.refs_2_.refs_1_), channel_id=1, source_target_pairs={{0,508},{4,0},{8,4},{12,8},{16,12},{20,16},{24,20},{28,24},{32,28}... | collective-permute-start | bytes 786440 | tf_op jit(solution)/shard_map/ppermute | solution.py:41
  29.7 0.0 copy-done.3
  29.7 0.1 copy.12.offsets_ref
  29.9 0.0 collective-permute-done.1.refs_3_.refs_2_
  29.9 5.5 %collective-permute-start.4 = (bf16[64,2048]{1,0:T(8,128)(2,1)S(1)}, bf16[64,2048]{1,0:T(8,128)(2,1)S(1)}, u32[]{:S(2)}, u32[]{:S(2)}) collective-permute-start(bf16[64,2048]{1,0:T(8,128)(2,1)S(1)} %collective-permute-done.1.refs_3_.refs_2_), channel_id=1, source_target_pairs={{0,508},{4,0},{8,4},{12,8},{16,12},{20,16},{24,20},{28,24},{32,28}... | collective-permute-start | bytes 786440 | tf_op jit(solution)/shard_map/ppermute | solution.py:41
  35.3 0.0 collective-permute-done.2.refs_4_.refs_3_
  35.4 1.9 %terms.2 = (bf16[64,2048]{1,0:T(8,128)(2,1)S(1)}, bf16[64,2048]{1,0:T(8,128)(2,1)S(1)}, bf16[64,2048]{1,0:T(8,128)(2,1)S(1)}, bf16[64,2048]{1,0:T(8,128)(2,1)S(1)}) custom-call(s32[1]{0:T(128)} %bitcast.4.index_ref, s32[4,4,2]{2,1,0:T(4,128)S(1)} %copy.12.offsets_ref, bf16[64,2048]{1,0:T(8,128)(2,1)S(1)} %get-tuple-element.50.refs_0_, ...), custom_call_target="tpu_custom_call" | custom-call | flops 1024 | bytes 1024 | tf_op jit(solution)/shard_map/terms/pallas_call | solution.py:129
  37.3 3.7 %collective-permute-start.3 = (bf16[64,2048]{1,0:T(8,128)(2,1)S(1)}, bf16[64,2048]{1,0:T(8,128)(2,1)S(1)}, u32[]{:S(2)}, u32[]{:S(2)}) collective-permute-start(bf16[64,2048]{1,0:T(8,128)(2,1)S(1)} %get-tuple-element.31), channel_id=1, source_target_pairs={{0,1},{1,0},{2,3},{3,2},{4,5},{5,4},{6,7},{7,6},{8,9},{9,8},{10,11... | collective-permute-start | bytes 786440 | tf_op jit(solution)/shard_map/ppermute | solution.py:45
  41.1 0.0 collective-permute-done.4.refs_4_
  41.1 1.1 %collective-permute-done.3 = bf16[64,2048]{1,0:T(8,128)(2,1)S(1)} collective-permute-done((bf16[64,2048]{1,0:T(8,128)(2,1)S(1)}, bf16[64,2048]{1,0:T(8,128)(2,1)S(1)}, u32[]{:S(2)}, u32[]{:S(2)}) %collective-permute-start.3) | collective-permute-done | bytes 262176 | tf_op jit(solution)/shard_map/ppermute | solution.py:45
  42.2 0.1 add_convert_fusion.1
  42.3 4.5 %collective-permute-start.5 = (bf16[64,2048]{1,0:T(8,128)(2,1)S(1)}, bf16[64,2048]{1,0:T(8,128)(2,1)S(1)}, u32[]{:S(2)}, u32[]{:S(2)}) collective-permute-start(bf16[64,2048]{1,0:T(8,128)(2,1)S(1)} %add_convert_fusion.1), channel_id=1, source_target_pairs={{0,2},{1,3},{2,0},{3,1},{4,6},{5,7},{6,4},{7,5},{8,10},{9,11},{10,... | collective-permute-start | bytes 786440 | tf_op jit(solution)/shard_map/ppermute | solution.py:49
  46.8 2.0 %terms.3 = (bf16[64,2048]{1,0:T(8,128)(2,1)S(1)}, bf16[64,2048]{1,0:T(8,128)(2,1)S(1)}, bf16[64,2048]{1,0:T(8,128)(2,1)S(1)}, bf16[64,2048]{1,0:T(8,128)(2,1)S(1)}) custom-call(s32[1]{0:T(128)} %bitcast.4.index_ref, s32[4,4,2]{2,1,0:T(4,128)S(1)} %copy.12.offsets_ref, bf16[64,2048]{1,0:T(8,128)(2,1)S(1)} %get-tuple-element.49.refs_1_.refs_0_, ...), custom_call_target="tpu_custom_call" | custom-call | flops 1024 | bytes 1024 | tf_op jit(solution)/shard_map/terms/pallas_call | solution.py:129
  48.8 2.6 %collective-permute-start.6 = (bf16[64,2048]{1,0:T(8,128)(2,1)S(1)}, bf16[64,2048]{1,0:T(8,128)(2,1)S(1)}, u32[]{:S(2)}, u32[]{:S(2)}) collective-permute-start(bf16[64,2048]{1,0:T(8,128)(2,1)S(1)} %get-tuple-element.38), channel_id=1, source_target_pairs={{0,1},{1,0},{2,3},{3,2},{4,5},{5,4},{6,7},{7,6},{8,9},{9,8},{10,11... | collective-permute-start | bytes 786440 | tf_op jit(solution)/shard_map/ppermute | solution.py:45
  51.4 1.8 %collective-permute-done.5.refs_4_ = bf16[64,2048]{1,0:T(8,128)(2,1)S(1)} collective-permute-done((bf16[64,2048]{1,0:T(8,128)(2,1)S(1)}, bf16[64,2048]{1,0:T(8,128)(2,1)S(1)}, u32[]{:S(2)}, u32[]{:S(2)}) %collective-permute-start.5) | collective-permute-done | bytes 262176 | tf_op jit(solution)/shard_map/ppermute | solution.py:49
  53.2 0.0 copy-start
  53.2 0.0 collective-permute-done.6
  53.2 0.1 add_convert_fusion
  53.3 4.5 %collective-permute-start.7 = (bf16[64,2048]{1,0:T(8,128)(2,1)S(1)}, bf16[64,2048]{1,0:T(8,128)(2,1)S(1)}, u32[]{:S(2)}, u32[]{:S(2)}) collective-permute-start(bf16[64,2048]{1,0:T(8,128)(2,1)S(1)} %add_convert_fusion), channel_id=1, source_target_pairs={{0,2},{1,3},{2,0},{3,1},{4,6},{5,7},{6,4},{7,5},{8,10},{9,11},{10,... | collective-permute-start | bytes 786440 | tf_op jit(solution)/shard_map/ppermute | solution.py:49
  57.8 3.4 %collective-permute-start.8 = (bf16[64,2048]{1,0:T(8,128)(2,1)S(1)}, bf16[64,2048]{1,0:T(8,128)(2,1)S(1)}, u32[]{:S(2)}, u32[]{:S(2)}) collective-permute-start(bf16[64,2048]{1,0:T(8,128)(2,1)S(1)} %get-tuple-element.45), channel_id=1, source_target_pairs={{0,1},{1,0},{2,3},{3,2},{4,5},{5,4},{6,7},{7,6},{8,9},{9,8},{10,11... | collective-permute-start | bytes 786440 | tf_op jit(solution)/shard_map/ppermute | solution.py:45
  61.2 1.9 %collective-permute-start.9 = (bf16[64,2048]{1,0:T(8,128)(2,1)S(1)}, bf16[64,2048]{1,0:T(8,128)(2,1)S(1)}, u32[]{:S(2)}, u32[]{:S(2)}) collective-permute-start(bf16[64,2048]{1,0:T(8,128)(2,1)S(1)} %get-tuple-element.46), channel_id=1, source_target_pairs={{0,1},{1,0},{2,3},{3,2},{4,5},{5,4},{6,7},{7,6},{8,9},{9,8},{10,11... | collective-permute-start | bytes 786440 | tf_op jit(solution)/shard_map/ppermute | solution.py:45
  63.1 0.1 collective-permute-done.7.refs_5_
  63.3 0.0 collective-permute-done.8.refs_2_
  63.3 1.4 %collective-permute-done.9.refs_3_ = bf16[64,2048]{1,0:T(8,128)(2,1)S(1)} collective-permute-done((bf16[64,2048]{1,0:T(8,128)(2,1)S(1)}, bf16[64,2048]{1,0:T(8,128)(2,1)S(1)}, u32[]{:S(2)}, u32[]{:S(2)}) %collective-permute-start.9) | collective-permute-done | bytes 262176 | tf_op jit(solution)/shard_map/ppermute | solution.py:45
  64.6 0.0 copy-done
  64.6 4.6 %spots.1 = bf16[128,2048]{1,0:T(8,128)(2,1)} custom-call(bf16[768,256]{1,0:T(8,128)(2,1)S(1)} %bitcast.10, bf16[256,256]{1,0:T(8,128)(2,1)S(1)} %copy-done, f32[7,2048]{1,0:T(8,128)S(1)} %pad_maximum_fusion.column_ref, bf16[64,2048]{1,0:T(8,128)(2,1)S(1)} %get-tuple-element.41.refs_0_, bf16[64,2048]{1,0:T(8,128)(2,1)S(1)} %get-tuple-element.42.refs_1_, ...), custom_call_target="tpu_custom_call" | custom-call | tf_op jit(solution)/shard_map/spots/pallas_call | solution.py:207
  (5 shorter events, 0.1 us)
Async XLA Ops:
  0.0 19.1 %copy-start.5 = (f32[3]{0:T(128)S(1)}, f32[3]{0:T(128)}, u32[]{:S(2)}) copy-start(f32[3]{0:T(128)} %param.14) | copy-start | bytes 40
  0.0 20.4 %copy-start.6 = (s32[1,16]{1,0:T(1,128)S(1)}, s32[1,16]{1,0:T(1,128)}, u32[]{:S(2)}) copy-start(s32[1,16]{1,0:T(1,128)} %param.12) | copy-start | bytes 196
  0.0 20.4 %copy-start.4 = (f32[3]{0:T(128)S(1)}, f32[3]{0:T(128)}, u32[]{:S(2)}) copy-start(f32[3]{0:T(128)} %param.13) | copy-start | bytes 40
  0.0 20.9 %copy-start.2 = (f32[128,128]{1,0:T(8,128)S(1)}, f32[128,128]{1,0:T(8,128)}, u32[]{:S(2)}) copy-start(f32[128,128]{1,0:T(8,128)} %constant.35) | copy-start | bytes 196612
  1.1 19.7 %copy-start.1 = (f32[128,128]{1,0:T(8,128)S(1)}, f32[128,128]{1,0:T(8,128)}, u32[]{:S(2)}) copy-start(f32[128,128]{1,0:T(8,128)} %constant.36) | copy-start | bytes 196612
  1.2 20.3 %collective-permute-start = (bf16[64,2048]{1,0:T(8,128)(2,1)S(1)}, bf16[64,2048]{1,0:T(8,128)(2,1)S(1)}, u32[]{:S(2)}, u32[]{:S(2)}) collective-permute-start(bf16[64,2048]{1,0:T(8,128)(2,1)S(1)} %get-tuple-element.50.refs_0_), channel_id=1, source_target_pairs={{0,508},{4,0},{8,4},{12,8},{16,12},{20,16},{24,20},{28,24},{32,28}... | collective-permute-start | bytes 786440 | tf_op jit(solution)/shard_map/ppermute | solution.py:41
  16.5 13.4 %collective-permute-start.1 = (bf16[64,2048]{1,0:T(8,128)(2,1)S(1)}, bf16[64,2048]{1,0:T(8,128)(2,1)S(1)}, u32[]{:S(2)}, u32[]{:S(2)}) collective-permute-start(bf16[64,2048]{1,0:T(8,128)(2,1)S(1)} %get-tuple-element.49.refs_1_.refs_0_), channel_id=1, source_target_pairs={{0,508},{4,0},{8,4},{12,8},{16,12},{20,16},{24,20},{28,24},{32,28}... | collective-permute-start | bytes 786440 | tf_op jit(solution)/shard_map/ppermute | solution.py:41
  21.1 8.6 %copy-start.3 = (s32[4,4,2]{1,2,0:T(2,128)S(1)}, s32[4,4,2]{1,2,0:T(2,128)}, u32[]{:S(2)}) copy-start(s32[4,4,2]{1,2,0:T(2,128)} %param.11) | copy-start | bytes 388
  21.4 13.9 %collective-permute-start.2 = (bf16[64,2048]{1,0:T(8,128)(2,1)S(1)}, bf16[64,2048]{1,0:T(8,128)(2,1)S(1)}, u32[]{:S(2)}, u32[]{:S(2)}) collective-permute-start(bf16[64,2048]{1,0:T(8,128)(2,1)S(1)} %collective-permute-done.refs_2_.refs_1_), channel_id=1, source_target_pairs={{0,508},{4,0},{8,4},{12,8},{16,12},{20,16},{24,20},{28,24},{32,28}... | collective-permute-start | bytes 786440 | tf_op jit(solution)/shard_map/ppermute | solution.py:41
  29.9 11.2 %collective-permute-start.4 = (bf16[64,2048]{1,0:T(8,128)(2,1)S(1)}, bf16[64,2048]{1,0:T(8,128)(2,1)S(1)}, u32[]{:S(2)}, u32[]{:S(2)}) collective-permute-start(bf16[64,2048]{1,0:T(8,128)(2,1)S(1)} %collective-permute-done.1.refs_3_.refs_2_), channel_id=1, source_target_pairs={{0,508},{4,0},{8,4},{12,8},{16,12},{20,16},{24,20},{28,24},{32,28}... | collective-permute-start | bytes 786440 | tf_op jit(solution)/shard_map/ppermute | solution.py:41
  37.3 4.9 %collective-permute-start.3 = (bf16[64,2048]{1,0:T(8,128)(2,1)S(1)}, bf16[64,2048]{1,0:T(8,128)(2,1)S(1)}, u32[]{:S(2)}, u32[]{:S(2)}) collective-permute-start(bf16[64,2048]{1,0:T(8,128)(2,1)S(1)} %get-tuple-element.31), channel_id=1, source_target_pairs={{0,1},{1,0},{2,3},{3,2},{4,5},{5,4},{6,7},{7,6},{8,9},{9,8},{10,11... | collective-permute-start | bytes 786440 | tf_op jit(solution)/shard_map/ppermute | solution.py:45
  42.3 10.9 %collective-permute-start.5 = (bf16[64,2048]{1,0:T(8,128)(2,1)S(1)}, bf16[64,2048]{1,0:T(8,128)(2,1)S(1)}, u32[]{:S(2)}, u32[]{:S(2)}) collective-permute-start(bf16[64,2048]{1,0:T(8,128)(2,1)S(1)} %add_convert_fusion.1), channel_id=1, source_target_pairs={{0,2},{1,3},{2,0},{3,1},{4,6},{5,7},{6,4},{7,5},{8,10},{9,11},{10,... | collective-permute-start | bytes 786440 | tf_op jit(solution)/shard_map/ppermute | solution.py:49
  48.8 4.4 %collective-permute-start.6 = (bf16[64,2048]{1,0:T(8,128)(2,1)S(1)}, bf16[64,2048]{1,0:T(8,128)(2,1)S(1)}, u32[]{:S(2)}, u32[]{:S(2)}) collective-permute-start(bf16[64,2048]{1,0:T(8,128)(2,1)S(1)} %get-tuple-element.38), channel_id=1, source_target_pairs={{0,1},{1,0},{2,3},{3,2},{4,5},{5,4},{6,7},{7,6},{8,9},{9,8},{10,11... | collective-permute-start | bytes 786440 | tf_op jit(solution)/shard_map/ppermute | solution.py:45
  53.2 11.4 %copy-start = (bf16[256,256]{1,0:T(8,128)(2,1)S(1)}, bf16[256,256]{1,0:T(8,128)(2,1)}, u32[]{:S(2)}) copy-start(bf16[256,256]{1,0:T(8,128)(2,1)} %constant.32.clone.right_ref) | copy-start | bytes 393220
  53.3 10.0 %collective-permute-start.7 = (bf16[64,2048]{1,0:T(8,128)(2,1)S(1)}, bf16[64,2048]{1,0:T(8,128)(2,1)S(1)}, u32[]{:S(2)}, u32[]{:S(2)}) collective-permute-start(bf16[64,2048]{1,0:T(8,128)(2,1)S(1)} %add_convert_fusion), channel_id=1, source_target_pairs={{0,2},{1,3},{2,0},{3,1},{4,6},{5,7},{6,4},{7,5},{8,10},{9,11},{10,... | collective-permute-start | bytes 786440 | tf_op jit(solution)/shard_map/ppermute | solution.py:49
  57.8 5.5 %collective-permute-start.8 = (bf16[64,2048]{1,0:T(8,128)(2,1)S(1)}, bf16[64,2048]{1,0:T(8,128)(2,1)S(1)}, u32[]{:S(2)}, u32[]{:S(2)}) collective-permute-start(bf16[64,2048]{1,0:T(8,128)(2,1)S(1)} %get-tuple-element.45), channel_id=1, source_target_pairs={{0,1},{1,0},{2,3},{3,2},{4,5},{5,4},{6,7},{7,6},{8,9},{9,8},{10,11... | collective-permute-start | bytes 786440 | tf_op jit(solution)/shard_map/ppermute | solution.py:45
  61.2 3.4 %collective-permute-start.9 = (bf16[64,2048]{1,0:T(8,128)(2,1)S(1)}, bf16[64,2048]{1,0:T(8,128)(2,1)S(1)}, u32[]{:S(2)}, u32[]{:S(2)}) collective-permute-start(bf16[64,2048]{1,0:T(8,128)(2,1)S(1)} %get-tuple-element.46), channel_id=1, source_target_pairs={{0,1},{1,0},{2,3},{3,2},{4,5},{5,4},{6,7},{7,6},{8,9},{9,8},{10,11... | collective-permute-start | bytes 786440 | tf_op jit(solution)/shard_map/ppermute | solution.py:45

commit v3 on v2

--- a/solution.py
+++ b/solution.py
@@ -19,6 +19,7 @@
 DIRS = 4
 
 CUTS = (0, 64, 128)
+SIDES = (0, 1024, 2048)
 FINAL_COLS = 512
 LANES = 128
 GROUP = 256
@@ -49,9 +50,12 @@
     return lax.ppermute(value, "dir", [(0, 2), (1, 3), (2, 0), (3, 1)])
 
 
-def term_kernel(first, rows, depths, index_ref, offsets_ref, *refs):
+def term_kernel(first, rows, depths, carried, index_ref, offsets_ref, *refs):
     blocks = refs[: len(depths)]
-    outs = refs[len(depths) :]
+    outs = refs[len(depths) + carried :]
+    if carried:
+        outs[2][2] = refs[len(depths)][...]
+        outs = (outs[0], outs[1], outs[2].at[1], outs[2].at[0])
     total = sum(depths)
     own = index_ref[0]
     wanted = (own, own ^ 2, own ^ 1, own ^ 3)
@@ -122,19 +126,22 @@
         finish(place, count - 1, turns[count - 1][place], turns[0][place])
 
 
-def terms(first, rows, index, offsets, blocks):
+def terms(first, rows, index, offsets, blocks, carried=()):
     depths = tuple(b.shape[0] for b in blocks)
     flat = jax.ShapeDtypeStruct((rows, PCOLS), jnp.bfloat16)
+    deep = jax.ShapeDtypeStruct((3, rows, PCOLS), jnp.bfloat16)
+    outs = (flat, flat, deep) if carried else (flat,) * DIRS
     whole = pl.BlockSpec(memory_space=pltpu.VMEM)
     return pl.pallas_call(
-        functools.partial(term_kernel, first, rows, depths),
-        out_shape=(flat,) * DIRS,
-        in_specs=[pl.BlockSpec(memory_space=pltpu.SMEM)] * 2 + [whole] * len(blocks),
-        out_specs=(whole,) * DIRS,
+        functools.partial(term_kernel, first, rows, depths, len(carried)),
+        out_shape=outs,
+        in_specs=[pl.BlockSpec(memory_space=pltpu.SMEM)] * 2
+        + [whole] * (len(blocks) + len(carried)),
+        out_specs=(whole,) * len(outs),
         compiler_params=pltpu.CompilerParams(vmem_limit_bytes=VMEM_LIMIT),
         cost_estimate=pl.CostEstimate(flops=1024, bytes_accessed=1024, transcendentals=0),
         name="terms",
-    )(index, offsets, *blocks)
+    )(index, offsets, *blocks, *carried)
 
 
 def series():
@@ -156,13 +163,13 @@
     return value
 
 
-def final_kernel(chunks, left_ref, right_ref, column_ref, *refs):
+def final_kernel(chunks, grown, left_ref, right_ref, column_ref, *refs):
     keeps, pairs, fars = refs[:chunks], refs[chunks : 2 * chunks], refs[2 * chunks : 3 * chunks]
-    out_ref = refs[3 * chunks]
+    out_ref = refs[3 * chunks + grown]
     cols = out_ref.shape[1]
     phase = jnp.concatenate(
         [
-            (k[...].astype(jnp.float32) + p[...].astype(jnp.float32)) + f[...].astype(jnp.float32)
+            (k[...].astype(jnp.float32) + p[0].astype(jnp.float32)) + f[...].astype(jnp.float32)
             for k, p, f in zip(keeps, pairs, fars)
         ],
         0,
@@ -201,23 +208,38 @@
         out_ref[:, at] = (total * lit).astype(jnp.bfloat16)
 
 
-def spots_of(left, right, column, keeps, pairs, fars):
+def spots_of(left, right, column, keeps, pair, fars, start, width, whole):
     chunks = len(keeps)
-    flat = [pl.BlockSpec((k.shape[0], FINAL_COLS), lambda i: (0, i)) for k in keeps]
+    step = min(FINAL_COLS, width)
+    at = start // step
+
+    def part(array):
+        skip = at if array.shape[1] == PCOLS else 0
+        return pl.BlockSpec((array.shape[0], step), lambda i: (0, i + skip))
+
+    deep = [
+        pl.BlockSpec((1, pair.shape[1], step), lambda i, place=place: (place, 0, i + at))
+        for place in (2, 1)
+    ]
+    taken = [column, *keeps, pair, pair, *fars]
+    specs = [part(column), *map(part, keeps), *deep, *map(part, fars)]
+    grown = [] if whole is None else [whole]
     return pl.pallas_call(
-        functools.partial(final_kernel, chunks),
-        grid=(PCOLS // FINAL_COLS,),
+        functools.partial(final_kernel, chunks, len(grown)),
+        grid=(width // step,),
         out_shape=jax.ShapeDtypeStruct((SPOT, PCOLS), jnp.bfloat16),
         in_specs=[
             pl.BlockSpec(left.shape, lambda i: (0, 0)),
             pl.BlockSpec(right.shape, lambda i: (0, 0)),
-            pl.BlockSpec((2 * SLICES + 1, FINAL_COLS), lambda i: (0, i)),
-        ]
-        + flat * 3,
-        out_specs=pl.BlockSpec((SPOT, FINAL_COLS), lambda i: (0, i)),
+            *specs,
+            *(pl.BlockSpec(memory_space=pl.ANY) for _ in grown),
+        ],
+        out_specs=pl.BlockSpec((SPOT, step), lambda i: (0, i + at)),
+        input_output_aliases={2 + len(taken): 0} if grown else {},
         compiler_params=pltpu.CompilerParams(vmem_limit_bytes=VMEM_LIMIT),
+        cost_estimate=pl.CostEstimate(flops=1024, bytes_accessed=1024, transcendentals=0),
         name="spots",
-    )(left, right, column, *keeps, *pairs, *fars)
+    )(left, right, *taken, *grown)
 
 
 def shards(layers, offsets, subap_valid, defocus, weights):
@@ -225,7 +247,7 @@
     tile = lax.axis_index("tile")
     total_rows = lax.axis_size("tile") * SUBPIX
     block = layers[0]
-    own = [block[a:b] for a, b in zip(CUTS, CUTS[1:])]
+    own = [block[: CUTS[1]], lax.optimization_barrier(block)[CUTS[1] :]]
     once = [shifted(piece, -1) for piece in own]
 
     real_part, imag_part, right = tables()
@@ -259,21 +281,20 @@
     joined = other_core(cross_send)
     joined, twice[1] = lax.optimization_barrier((joined, twice[1]))
     both = (send.astype(jnp.float32) + joined.astype(jnp.float32)).astype(jnp.bfloat16)
-    both, twice[1] = lax.optimization_barrier((both, twice[1]))
-    keeps, crosses, fars = [keep], [cross], [other_chip(both)]
+    keeps, fars = [keep], [other_chip(both)]
 
     blocks = own[1:] + once + twice
-    keep, send, cross, cross_send = terms(CUTS[1], CUTS[2] - CUTS[1], index, offsets, blocks)
-    joined = other_core(cross_send)
-    send, fars[0] = lax.optimization_barrier((send, fars[0]))
-    both = (send.astype(jnp.float32) + joined.astype(jnp.float32)).astype(jnp.bfloat16)
-    crosses.append(cross)
+    keep, send, crosses = terms(CUTS[1], CUTS[2] - CUTS[1], index, offsets, blocks, (cross,))
     keeps.append(keep)
-    fars.append(other_chip(both))
-    crosses[0], crosses[1], both = lax.optimization_barrier((crosses[0], crosses[1], both))
-    pairs = [other_core(cross) for cross in crosses]
-    fars[1], column = lax.optimization_barrier((fars[1], column))
-    spots = spots_of(left, right, column, keeps, pairs, fars)
+    pair = other_core(crosses)
+    sides = []
+    for a, b in zip(SIDES, SIDES[1:]):
+        both = send[:, a:b].astype(jnp.float32) + pair[0, :, a:b].astype(jnp.float32)
+        sides.append(other_chip(both.astype(jnp.bfloat16)))
+
+    spots = None
+    for side, a, b in zip(sides, SIDES, SIDES[1:]):
+        spots = spots_of(left, right, column, keeps, pair, fars + [side], a, b - a, spots)
     return spots[None, None]
 
 

time: 69.7 us -> 66.2 us (0.950)
  starting transfers between devices: 52.4 us -> 49.1 us
  waiting for transfers between devices: 4.75 us -> 3.88 us
  Pallas kernels: 8.51 us -> 9.22 us
    ppermute x4 -> x2, starting transfers between devices: 11.6 us -> 6.01 us  [other_core(): return lax.ppermute(value, 'dir', [(0, 1), (1, 0), (2, 3), (3, 2)])]
    ppermute x2 -> x3, starting transfers between devices: 9.07 us -> 11.3 us  [other_chip(): return lax.ppermute(value, 'dir', [(0, 2), (1, 3), (2, 0), (3, 1)])]
    ppermute x4 -> x2, waiting for transfers between devices: 2.5 us -> 1.13 us  [other_core(): return lax.ppermute(value, 'dir', [(0, 1), (1, 0), (2, 3), (3, 2)])]
    ppermute x2 -> x3, waiting for transfers between devices: 1.97 us -> 2.69 us  [other_chip(): return lax.ppermute(value, 'dir', [(0, 2), (1, 3), (2, 0), (3, 1)])]
    pallas_call x3 -> x4, Pallas kernels: 8.51 us -> 9.22 us  [the longest x2 5.27 us: spots_of(): pl.pallas_call(functools.partial(final_kernel, chunks, len(grown)), grid=...]
  transfers between devices with their start and end apart: 10 -> 9, of which waited for: 5 -> 3; matrix products, arithmetic and copies ran while one was open for 3% -> 3% of each run, Pallas kernels for 6% -> 7%
where the time goes in v3:
time: 66.2 us; the launch traced here: 65.7 us
  starting transfers between devices  49.1 us (74%)
  Pallas kernels  9.22 us (14%)
  waiting for transfers between devices  3.88 us (6%)
  other arithmetic  1.98 us (3%)
  local copies, waits for them, and re-layouts  1.29 us (2%)
    ppermute x4, starting transfers between devices, shifted(): lax.ppermute(value, 'tile', [(i, (i + by) % count) for i in range(count)])  31.7 us
    ppermute x3, starting transfers between devices, other_chip(): return lax.ppermute(value, 'dir', [(0, 2), (1, 3), (2, 0), (3, 1)])  11.3 us
    ppermute x2, starting transfers between devices, other_core(): return lax.ppermute(value, 'dir', [(0, 1), (1, 0), (2, 3), (3, 2)])  6.01 us
    pallas_call x2, Pallas kernels, spots_of(): pl.pallas_call(functools.partial(final_kernel, chunks, len(grown)), grid=...  5.27 us
    pallas_call x2, Pallas kernels, terms(): pl.pallas_call(functools.partial(term_kernel, first, rows, depths, len(ca...  3.95 us
    ppermute x3, waiting for transfers between devices, other_chip(): return lax.ppermute(value, 'dir', [(0, 2), (1, 3), (2, 0), (3, 1)])  2.69 us
  transfers between devices with their start and end apart: 9, of which 3 were waited for; matrix products, arithmetic and copies ran while one was open for 3% of the time, Pallas kernels for 7%

profile of v3, /device:TPU:1, one launch (start us, length us, event | category | flops | bytes accessed | tf_op | source)
XLA Modules:
  0.0 65.7 jit_solution(8861352839435506952)
XLA Ops:
  0.0 0.0 copy-start.1
  0.0 1.0 %slice_bitcast_fusion.refs_0_ = bf16[64,2048]{1,0:T(8,128)(2,1)S(1)} fusion(bf16[1,128,2048]{2,1,0:T(8,128)(2,1)} %param.10), kind=kLoop, calls=%fused_computation.6 | loop fusion | bytes 524288 | tf_op jit(solution)/shard_map/slice | solution.py:250
  1.0 15.2 %collective-permute-start = (bf16[64,2048]{1,0:T(8,128)(2,1)S(1)}, bf16[64,2048]{1,0:T(8,128)(2,1)S(1)}, u32[]{:S(2)}, u32[]{:S(2)}) collective-permute-start(bf16[64,2048]{1,0:T(8,128)(2,1)S(1)} %slice_bitcast_fusion.refs_0_), channel_id=1, source_target_pairs={{0,508},{4,0},{8,4},{12,8},{16,12},{20,16},{24,20},{28,24},{32,28}... | collective-permute-start | bytes 786440 | tf_op jit(solution)/shard_map/ppermute | solution.py:42
  16.2 0.0 copy-done.1
  16.2 0.0 copy-start.6
  16.2 0.0 copy-start.7
  16.2 0.0 copy-start.5
  16.3 0.0 copy-start.3
  16.3 0.0 copy-start.2
  16.3 2.8 %collective-permute-start.1 = (bf16[64,2048]{1,0:T(8,128)(2,1)S(1)}, bf16[64,2048]{1,0:T(8,128)(2,1)S(1)}, u32[]{:S(2)}, u32[]{:S(2)}) collective-permute-start(bf16[64,2048]{1,0:T(8,128)(2,1)S(1)} %slice.28.refs_1_.refs_0_), channel_id=1, source_target_pairs={{0,508},{4,0},{8,4},{12,8},{16,12},{20,16},{24,20},{28,24},{32,28}... | collective-permute-start | bytes 786440 | tf_op jit(solution)/shard_map/ppermute | solution.py:42
  19.1 0.0 copy-done.6
  19.1 0.6 reduce_sum.9
  19.7 0.7 divide_sqrt_fusion
  20.4 0.0 copy-done.7
  20.4 0.0 copy-done.5
  20.4 0.1 multiply_cosine_fusion.1
  20.5 0.3 fusion.3
  20.9 0.0 copy-done.3
  20.9 0.0 copy-done.2
  20.9 0.1 negate_convert_fusion
  21.0 0.1 broadcast_in_dim.8
  21.1 0.0 copy-start.4
  21.1 0.0 collective-permute-done.refs_2_.refs_1_
  21.2 8.3 %collective-permute-start.2 = (bf16[64,2048]{1,0:T(8,128)(2,1)S(1)}, bf16[64,2048]{1,0:T(8,128)(2,1)S(1)}, u32[]{:S(2)}, u32[]{:S(2)}) collective-permute-start(bf16[64,2048]{1,0:T(8,128)(2,1)S(1)} %collective-permute-done.refs_2_.refs_1_), channel_id=1, source_target_pairs={{0,508},{4,0},{8,4},{12,8},{16,12},{20,16},{24,20},{28,24},{32,28}... | collective-permute-start | bytes 786440 | tf_op jit(solution)/shard_map/ppermute | solution.py:42
  29.5 0.0 copy-done.4
  29.5 0.1 copy.12.offsets_ref
  29.6 0.0 collective-permute-done.1.refs_3_.refs_2_
  29.6 5.5 %collective-permute-start.4 = (bf16[64,2048]{1,0:T(8,128)(2,1)S(1)}, bf16[64,2048]{1,0:T(8,128)(2,1)S(1)}, u32[]{:S(2)}, u32[]{:S(2)}) collective-permute-start(bf16[64,2048]{1,0:T(8,128)(2,1)S(1)} %collective-permute-done.1.refs_3_.refs_2_), channel_id=1, source_target_pairs={{0,508},{4,0},{8,4},{12,8},{16,12},{20,16},{24,20},{28,24},{32,28}... | collective-permute-start | bytes 786440 | tf_op jit(solution)/shard_map/ppermute | solution.py:42
  35.1 0.0 collective-permute-done.2.refs_4_.refs_3_
  35.1 1.9 %terms.2 = (bf16[64,2048]{1,0:T(8,128)(2,1)S(1)}, bf16[64,2048]{1,0:T(8,128)(2,1)S(1)}, bf16[64,2048]{1,0:T(8,128)(2,1)S(1)}, bf16[64,2048]{1,0:T(8,128)(2,1)S(1)}) custom-call(s32[1]{0:T(128)} %bitcast.4.index_ref, s32[4,4,2]{2,1,0:T(4,128)S(1)} %copy.12.offsets_ref, bf16[64,2048]{1,0:T(8,128)(2,1)S(1)} %slice_bitcast_fusion.refs_0_, ...), custom_call_target="tpu_custom_call" | custom-call | flops 1024 | bytes 1024 | tf_op jit(solution)/shard_map/terms/pallas_call | solution.py:135
  37.1 3.7 %collective-permute-start.3 = (bf16[64,2048]{1,0:T(8,128)(2,1)S(1)}, bf16[64,2048]{1,0:T(8,128)(2,1)S(1)}, u32[]{:S(2)}, u32[]{:S(2)}) collective-permute-start(bf16[64,2048]{1,0:T(8,128)(2,1)S(1)} %get-tuple-element.23), channel_id=1, source_target_pairs={{0,1},{1,0},{2,3},{3,2},{4,5},{5,4},{6,7},{7,6},{8,9},{9,8},{10,11... | collective-permute-start | bytes 786440 | tf_op jit(solution)/shard_map/ppermute | solution.py:46
  40.8 0.0 collective-permute-done.4.refs_4_
  40.8 1.1 %collective-permute-done.3 = bf16[64,2048]{1,0:T(8,128)(2,1)S(1)} collective-permute-done((bf16[64,2048]{1,0:T(8,128)(2,1)S(1)}, bf16[64,2048]{1,0:T(8,128)(2,1)S(1)}, u32[]{:S(2)}, u32[]{:S(2)}) %collective-permute-start.3) | collective-permute-done | bytes 262176 | tf_op jit(solution)/shard_map/ppermute | solution.py:46
  42.0 2.0 %terms.3 = (bf16[64,2048]{1,0:T(8,128)(2,1)S(1)}, bf16[64,2048]{1,0:T(8,128)(2,1)S(1)}, bf16[3,64,2048]{2,1,0:T(8,128)(2,1)S(1)}) custom-call(s32[1]{0:T(128)} %bitcast.4.index_ref, s32[4,4,2]{2,1,0:T(4,128)S(1)} %copy.12.offsets_ref, bf16[64,2048]{1,0:T(8,128)(2,1)S(1)} %slice.28.refs_1_.refs_0_, bf16[64,2048]{1,0:T(8,128)(2,1)S(1)} %collective-permute-done.refs_2_.refs_1_, ...), custom_call_target="tpu_custom_call" | custom-call | flops 1024 | bytes 1024 | tf_op jit(solution)/shard_map/terms/pallas_call | solution.py:135
  44.0 2.3 %collective-permute-start.5 = (bf16[3,64,2048]{2,1,0:T(8,128)(2,1)S(1)}, bf16[3,64,2048]{2,1,0:T(8,128)(2,1)S(1)}, u32[]{:S(2)}, u32[]{:S(2)}) collective-permute-start(bf16[3,64,2048]{2,1,0:T(8,128)(2,1)S(1)} %get-tuple-element.27), channel_id=1, source_target_pairs={{0,1},{1,0},{2,3},{3,2},{4,5},{5,4},{6,7},{7,6},{8,9},{9,8},{10,11... | collective-permute-start | bytes 2359304 | tf_op jit(solution)/shard_map/ppermute | solution.py:46
  46.2 0.1 add_convert_fusion
  46.3 4.5 %collective-permute-start.6 = (bf16[64,2048]{1,0:T(8,128)(2,1)S(1)}, bf16[64,2048]{1,0:T(8,128)(2,1)S(1)}, u32[]{:S(2)}, u32[]{:S(2)}) collective-permute-start(bf16[64,2048]{1,0:T(8,128)(2,1)S(1)} %add_convert_fusion), channel_id=1, source_target_pairs={{0,2},{1,3},{2,0},{3,1},{4,6},{5,7},{6,4},{7,5},{8,10},{9,11},{10,... | collective-permute-start | bytes 786440 | tf_op jit(solution)/shard_map/ppermute | solution.py:50
  50.9 0.0 collective-permute-done.5.refs_2_.refs_3_
  50.9 0.0 copy-start
  50.9 0.1 fusion
  51.0 2.2 %collective-permute-start.8 = (bf16[64,1024]{1,0:T(8,128)(2,1)S(1)}, bf16[64,1024]{1,0:T(8,128)(2,1)S(1)}, u32[]{:S(2)}, u32[]{:S(2)}) collective-permute-start(bf16[64,1024]{1,0:T(8,128)(2,1)S(1)} %get-tuple-element.31), channel_id=1, source_target_pairs={{0,2},{1,3},{2,0},{3,1},{4,6},{5,7},{6,4},{7,5},{8,10},{9,11},{10,... | collective-permute-start | bytes 393224 | tf_op jit(solution)/shard_map/ppermute | solution.py:50
  53.2 4.5 %collective-permute-start.7 = (bf16[64,1024]{1,0:T(8,128)(2,1)S(1)}, bf16[64,1024]{1,0:T(8,128)(2,1)S(1)}, u32[]{:S(2)}, u32[]{:S(2)}) collective-permute-start(bf16[64,1024]{1,0:T(8,128)(2,1)S(1)} %get-tuple-element.32), channel_id=1, source_target_pairs={{0,2},{1,3},{2,0},{3,1},{4,6},{5,7},{6,4},{7,5},{8,10},{9,11},{10,... | collective-permute-start | bytes 393224 | tf_op jit(solution)/shard_map/ppermute | solution.py:50
  57.8 0.0 collective-permute-done.6.refs_4_
  57.8 2.5 %collective-permute-done.8.refs_5_ = bf16[64,1024]{1,0:T(8,128)(2,1)S(1)} collective-permute-done((bf16[64,1024]{1,0:T(8,128)(2,1)S(1)}, bf16[64,1024]{1,0:T(8,128)(2,1)S(1)}, u32[]{:S(2)}, u32[]{:S(2)}) %collective-permute-start.8) | collective-permute-done | bytes 131104 | tf_op jit(solution)/shard_map/ppermute | solution.py:50
  60.3 0.0 copy-done
  60.3 2.6 %spots.2.refs_6_ = bf16[128,2048]{1,0:T(8,128)(2,1)} custom-call(bf16[768,256]{1,0:T(8,128)(2,1)S(1)} %bitcast.19, bf16[256,256]{1,0:T(8,128)(2,1)S(1)} %copy-done, f32[7,2048]{1,0:T(8,128)S(1)} %pad_maximum_fusion.column_ref, bf16[64,2048]{1,0:T(8,128)(2,1)S(1)} %get-tuple-element.22.refs_0_, bf16[64,2048]{1,0:T(8,128)(2,1)S(1)} %get-tuple-element.26.refs_1_, ...), custom_call_target="tpu_custom_call" | custom-call | flops 1024 | bytes 1024 | tf_op jit(solution)/shard_map/spots/pallas_call | solution.py:227
  62.9 0.2 collective-permute-done.7.refs_5_
  63.1 2.6 %spots.3 = bf16[128,2048]{1,0:T(8,128)(2,1)} custom-call(bf16[768,256]{1,0:T(8,128)(2,1)S(1)} %bitcast.20, bf16[256,256]{1,0:T(8,128)(2,1)S(1)} %copy-done, f32[7,2048]{1,0:T(8,128)S(1)} %pad_maximum_fusion.column_ref, bf16[64,2048]{1,0:T(8,128)(2,1)S(1)} %get-tuple-element.22.refs_0_, ...), custom_call_target="tpu_custom_call", output_to_operand_aliasing={{}: (9, {})} | custom-call | flops 1024 | bytes 1024 | tf_op jit(solution)/shard_map/spots/pallas_call | solution.py:227
  (6 shorter events, 0.1 us)
Async XLA Ops:
  0.0 16.2 %copy-start.1 = (bf16[1,128,2048]{2,1,0:T(8,128)(2,1)S(1)}, bf16[1,128,2048]{2,1,0:T(8,128)(2,1)}, u32[]{:S(2)}) copy-start(bf16[1,128,2048]{2,1,0:T(8,128)(2,1)} %param.10) | copy-start | bytes 1572868
  1.0 20.1 %collective-permute-start = (bf16[64,2048]{1,0:T(8,128)(2,1)S(1)}, bf16[64,2048]{1,0:T(8,128)(2,1)S(1)}, u32[]{:S(2)}, u32[]{:S(2)}) collective-permute-start(bf16[64,2048]{1,0:T(8,128)(2,1)S(1)} %slice_bitcast_fusion.refs_0_), channel_id=1, source_target_pairs={{0,508},{4,0},{8,4},{12,8},{16,12},{20,16},{24,20},{28,24},{32,28}... | collective-permute-start | bytes 786440 | tf_op jit(solution)/shard_map/ppermute | solution.py:42
  16.2 2.9 %copy-start.6 = (f32[3]{0:T(128)S(1)}, f32[3]{0:T(128)}, u32[]{:S(2)}) copy-start(f32[3]{0:T(128)} %param.14) | copy-start | bytes 40
  16.2 4.2 %copy-start.7 = (s32[1,16]{1,0:T(1,128)S(1)}, s32[1,16]{1,0:T(1,128)}, u32[]{:S(2)}) copy-start(s32[1,16]{1,0:T(1,128)} %param.12) | copy-start | bytes 196
  16.2 4.2 %copy-start.5 = (f32[3]{0:T(128)S(1)}, f32[3]{0:T(128)}, u32[]{:S(2)}) copy-start(f32[3]{0:T(128)} %param.13) | copy-start | bytes 40
  16.3 4.6 %copy-start.3 = (f32[128,128]{1,0:T(8,128)S(1)}, f32[128,128]{1,0:T(8,128)}, u32[]{:S(2)}) copy-start(f32[128,128]{1,0:T(8,128)} %constant.35) | copy-start | bytes 196612
  16.3 4.6 %copy-start.2 = (f32[128,128]{1,0:T(8,128)S(1)}, f32[128,128]{1,0:T(8,128)}, u32[]{:S(2)}) copy-start(f32[128,128]{1,0:T(8,128)} %constant.36) | copy-start | bytes 196612
  16.3 13.3 %collective-permute-start.1 = (bf16[64,2048]{1,0:T(8,128)(2,1)S(1)}, bf16[64,2048]{1,0:T(8,128)(2,1)S(1)}, u32[]{:S(2)}, u32[]{:S(2)}) collective-permute-start(bf16[64,2048]{1,0:T(8,128)(2,1)S(1)} %slice.28.refs_1_.refs_0_), channel_id=1, source_target_pairs={{0,508},{4,0},{8,4},{12,8},{16,12},{20,16},{24,20},{28,24},{32,28}... | collective-permute-start | bytes 786440 | tf_op jit(solution)/shard_map/ppermute | solution.py:42
  21.1 8.4 %copy-start.4 = (s32[4,4,2]{1,2,0:T(2,128)S(1)}, s32[4,4,2]{1,2,0:T(2,128)}, u32[]{:S(2)}) copy-start(s32[4,4,2]{1,2,0:T(2,128)} %param.11) | copy-start | bytes 388
  21.2 13.9 %collective-permute-start.2 = (bf16[64,2048]{1,0:T(8,128)(2,1)S(1)}, bf16[64,2048]{1,0:T(8,128)(2,1)S(1)}, u32[]{:S(2)}, u32[]{:S(2)}) collective-permute-start(bf16[64,2048]{1,0:T(8,128)(2,1)S(1)} %collective-permute-done.refs_2_.refs_1_), channel_id=1, source_target_pairs={{0,508},{4,0},{8,4},{12,8},{16,12},{20,16},{24,20},{28,24},{32,28}... | collective-permute-start | bytes 786440 | tf_op jit(solution)/shard_map/ppermute | solution.py:42
  29.6 11.2 %collective-permute-start.4 = (bf16[64,2048]{1,0:T(8,128)(2,1)S(1)}, bf16[64,2048]{1,0:T(8,128)(2,1)S(1)}, u32[]{:S(2)}, u32[]{:S(2)}) collective-permute-start(bf16[64,2048]{1,0:T(8,128)(2,1)S(1)} %collective-permute-done.1.refs_3_.refs_2_), channel_id=1, source_target_pairs={{0,508},{4,0},{8,4},{12,8},{16,12},{20,16},{24,20},{28,24},{32,28}... | collective-permute-start | bytes 786440 | tf_op jit(solution)/shard_map/ppermute | solution.py:42
  37.1 4.9 %collective-permute-start.3 = (bf16[64,2048]{1,0:T(8,128)(2,1)S(1)}, bf16[64,2048]{1,0:T(8,128)(2,1)S(1)}, u32[]{:S(2)}, u32[]{:S(2)}) collective-permute-start(bf16[64,2048]{1,0:T(8,128)(2,1)S(1)} %get-tuple-element.23), channel_id=1, source_target_pairs={{0,1},{1,0},{2,3},{3,2},{4,5},{5,4},{6,7},{7,6},{8,9},{9,8},{10,11... | collective-permute-start | bytes 786440 | tf_op jit(solution)/shard_map/ppermute | solution.py:46
  44.0 6.9 %collective-permute-start.5 = (bf16[3,64,2048]{2,1,0:T(8,128)(2,1)S(1)}, bf16[3,64,2048]{2,1,0:T(8,128)(2,1)S(1)}, u32[]{:S(2)}, u32[]{:S(2)}) collective-permute-start(bf16[3,64,2048]{2,1,0:T(8,128)(2,1)S(1)} %get-tuple-element.27), channel_id=1, source_target_pairs={{0,1},{1,0},{2,3},{3,2},{4,5},{5,4},{6,7},{7,6},{8,9},{9,8},{10,11... | collective-permute-start | bytes 2359304 | tf_op jit(solution)/shard_map/ppermute | solution.py:46
  46.3 11.4 %collective-permute-start.6 = (bf16[64,2048]{1,0:T(8,128)(2,1)S(1)}, bf16[64,2048]{1,0:T(8,128)(2,1)S(1)}, u32[]{:S(2)}, u32[]{:S(2)}) collective-permute-start(bf16[64,2048]{1,0:T(8,128)(2,1)S(1)} %add_convert_fusion), channel_id=1, source_target_pairs={{0,2},{1,3},{2,0},{3,1},{4,6},{5,7},{6,4},{7,5},{8,10},{9,11},{10,... | collective-permute-start | bytes 786440 | tf_op jit(solution)/shard_map/ppermute | solution.py:50
  50.9 9.4 %copy-start = (bf16[256,256]{1,0:T(8,128)(2,1)S(1)}, bf16[256,256]{1,0:T(8,128)(2,1)}, u32[]{:S(2)}) copy-start(bf16[256,256]{1,0:T(8,128)(2,1)} %constant.32.clone.right_ref) | copy-start | bytes 393220
  51.0 9.3 %collective-permute-start.8 = (bf16[64,1024]{1,0:T(8,128)(2,1)S(1)}, bf16[64,1024]{1,0:T(8,128)(2,1)S(1)}, u32[]{:S(2)}, u32[]{:S(2)}) collective-permute-start(bf16[64,1024]{1,0:T(8,128)(2,1)S(1)} %get-tuple-element.31), channel_id=1, source_target_pairs={{0,2},{1,3},{2,0},{3,1},{4,6},{5,7},{6,4},{7,5},{8,10},{9,11},{10,... | collective-permute-start | bytes 393224 | tf_op jit(solution)/shard_map/ppermute | solution.py:50
  53.2 9.9 %collective-permute-start.7 = (bf16[64,1024]{1,0:T(8,128)(2,1)S(1)}, bf16[64,1024]{1,0:T(8,128)(2,1)S(1)}, u32[]{:S(2)}, u32[]{:S(2)}) collective-permute-start(bf16[64,1024]{1,0:T(8,128)(2,1)S(1)} %get-tuple-element.32), channel_id=1, source_target_pairs={{0,2},{1,3},{2,0},{3,1},{4,6},{5,7},{6,4},{7,5},{8,10},{9,11},{10,... | collective-permute-start | bytes 393224 | tf_op jit(solution)/shard_map/ppermute | solution.py:50

commit v4 on v3

--- a/solution.py
+++ b/solution.py
@@ -20,8 +20,9 @@
 
 CUTS = (0, 64, 128)
 SIDES = (0, 1024, 2048)
-FINAL_COLS = 512
+FINAL_COLS = 1024
 LANES = 128
+BAND = 256
 GROUP = 256
 VMEM_LIMIT = 48 * 1024 * 1024
 
@@ -54,8 +55,8 @@
     blocks = refs[: len(depths)]
     outs = refs[len(depths) + carried :]
     if carried:
-        outs[2][2] = refs[len(depths)][...]
-        outs = (outs[0], outs[1], outs[2].at[1], outs[2].at[0])
+        outs[2][2 * rows :] = refs[len(depths)][...]
+        outs = (*outs[:2], outs[2].at[rows : 2 * rows], outs[2].at[:rows])
     total = sum(depths)
     own = index_ref[0]
     wanted = (own, own ^ 2, own ^ 1, own ^ 3)
@@ -129,8 +130,10 @@
 def terms(first, rows, index, offsets, blocks, carried=()):
     depths = tuple(b.shape[0] for b in blocks)
     flat = jax.ShapeDtypeStruct((rows, PCOLS), jnp.bfloat16)
-    deep = jax.ShapeDtypeStruct((3, rows, PCOLS), jnp.bfloat16)
-    outs = (flat, flat, deep) if carried else (flat,) * DIRS
+    outs = (flat,) * DIRS
+    if carried:
+        deep = 2 * rows + carried[0].shape[0]
+        outs = (flat, flat, jax.ShapeDtypeStruct((deep, PCOLS), jnp.bfloat16))
     whole = pl.BlockSpec(memory_space=pltpu.VMEM)
     return pl.pallas_call(
         functools.partial(term_kernel, first, rows, depths, len(carried)),
@@ -164,48 +167,51 @@
 
 
 def final_kernel(chunks, grown, left_ref, right_ref, column_ref, *refs):
-    keeps, pairs, fars = refs[:chunks], refs[chunks : 2 * chunks], refs[2 * chunks : 3 * chunks]
-    out_ref = refs[3 * chunks + grown]
-    cols = out_ref.shape[1]
-    phase = jnp.concatenate(
-        [
-            (k[...].astype(jnp.float32) + p[0].astype(jnp.float32)) + f[...].astype(jnp.float32)
-            for k, p, f in zip(keeps, pairs, fars)
-        ],
-        0,
-    )
-    turns = phase * (0.5 / math.pi)
-    turns = turns - jnp.round(turns)
-    square = turns * turns
-    field = jnp.concatenate(
-        [horner(COSINE, square), turns * horner(SINE, square)], 0
-    ).astype(jnp.bfloat16)
-    focal = jnp.dot(left_ref[...], field, preferred_element_type=jnp.float32)
-    reals, imags = [], []
-    for altitude in range(SLICES):
-        real = focal[2 * SPOT * altitude : 2 * SPOT * altitude + SPOT]
-        imag = focal[2 * SPOT * altitude + SPOT : 2 * SPOT * (altitude + 1)]
-        cosine = column_ref[altitude : altitude + 1]
-        sine = column_ref[SLICES + altitude : SLICES + altitude + 1]
-        reals.append((real * cosine - imag * sine).astype(jnp.bfloat16))
-        imags.append((real * sine + imag * cosine).astype(jnp.bfloat16))
-    real = jnp.concatenate(reals, 0)
-    imag = jnp.concatenate(imags, 0)
-    for place in range(cols // SUBPIX):
-        at = slice(place * SUBPIX, (place + 1) * SUBPIX)
-        spot = jnp.dot(
-            jnp.concatenate([real[:, at], imag[:, at]], 1),
-            right_ref[...],
-            preferred_element_type=jnp.float32,
+    keeps, pair_ref, fars = refs[:chunks], refs[chunks], refs[chunks + 1 : 2 * chunks + 1]
+    out_ref = refs[2 * chunks + 1 + grown]
+    last = keeps[1].shape[0]
+    pairs = (slice(2 * last, None), slice(last, 2 * last))
+    for at in range(0, out_ref.shape[1], BAND):
+        band = slice(at, at + BAND)
+        phase = jnp.concatenate(
+            [
+                (k[:, band].astype(jnp.float32) + pair_ref[p, band].astype(jnp.float32))
+                + f[:, band].astype(jnp.float32)
+                for k, p, f in zip(keeps, pairs, fars)
+            ],
+            0,
         )
-        power = spot * spot
-        power = power[:, :SPOT] + power[:, SPOT:]
-        total = None
+        turns = phase * (0.5 / math.pi)
+        turns = turns - jnp.round(turns)
+        square = turns * turns
+        field = jnp.concatenate(
+            [horner(COSINE, square), turns * horner(SINE, square)], 0
+        ).astype(jnp.bfloat16)
+        focal = jnp.dot(left_ref[...], field, preferred_element_type=jnp.float32)
+        reals, imags = [], []
         for altitude in range(SLICES):
-            piece = power[altitude * SPOT : (altitude + 1) * SPOT]
-            total = piece if total is None else total + piece
-        lit = column_ref[2 * SLICES : 2 * SLICES + 1, at]
-        out_ref[:, at] = (total * lit).astype(jnp.bfloat16)
+            real = focal[2 * SPOT * altitude : 2 * SPOT * altitude + SPOT]
+            imag = focal[2 * SPOT * altitude + SPOT : 2 * SPOT * (altitude + 1)]
+            cosine = column_ref[altitude : altitude + 1, band]
+            sine = column_ref[SLICES + altitude : SLICES + altitude + 1, band]
+            reals.append((real * cosine - imag * sine).astype(jnp.bfloat16))
+            imags.append((real * sine + imag * cosine).astype(jnp.bfloat16))
+        real = jnp.concatenate(reals, 0)
+        imag = jnp.concatenate(imags, 0)
+        for place in range(0, BAND, SUBPIX):
+            spot = jnp.dot(
+                jnp.concatenate([real[:, place : place + SUBPIX], imag[:, place : place + SUBPIX]], 1),
+                right_ref[...],
+                preferred_element_type=jnp.float32,
+            )
+            power = spot * spot
+            power = power[:, :SPOT] + power[:, SPOT:]
+            total = power[:SPOT]
+            for altitude in range(1, SLICES):
+                total = total + power[altitude * SPOT : (altitude + 1) * SPOT]
+            to = slice(at + place, at + place + SUBPIX)
+            lit = column_ref[2 * SLICES : 2 * SLICES + 1, to]
+            out_ref[:, to] = (total * lit).astype(jnp.bfloat16)
 
 
 def spots_of(left, right, column, keeps, pair, fars, start, width, whole):
@@ -217,12 +223,7 @@
         skip = at if array.shape[1] == PCOLS else 0
         return pl.BlockSpec((array.shape[0], step), lambda i: (0, i + skip))
 
-    deep = [
-        pl.BlockSpec((1, pair.shape[1], step), lambda i, place=place: (place, 0, i + at))
-        for place in (2, 1)
-    ]
-    taken = [column, *keeps, pair, pair, *fars]
-    specs = [part(column), *map(part, keeps), *deep, *map(part, fars)]
+    taken = [column, *keeps, pair, *fars]
     grown = [] if whole is None else [whole]
     return pl.pallas_call(
         functools.partial(final_kernel, chunks, len(grown)),
@@ -231,7 +232,7 @@
         in_specs=[
             pl.BlockSpec(left.shape, lambda i: (0, 0)),
             pl.BlockSpec(right.shape, lambda i: (0, 0)),
-            *specs,
+            *map(part, taken),
             *(pl.BlockSpec(memory_space=pl.ANY) for _ in grown),
         ],
         out_specs=pl.BlockSpec((SPOT, step), lambda i: (0, i + at)),
@@ -247,8 +248,8 @@
     tile = lax.axis_index("tile")
     total_rows = lax.axis_size("tile") * SUBPIX
     block = layers[0]
-    own = [block[: CUTS[1]], lax.optimization_barrier(block)[CUTS[1] :]]
-    once = [shifted(piece, -1) for piece in own]
+    own = [block[: CUTS[1]]]
+    once = [shifted(own[0], -1)]
 
     real_part, imag_part, right = tables()
     row = (
@@ -273,7 +274,10 @@
     lit = jnp.repeat(subap_valid.astype(jnp.float32), SUBPIX, axis=1)
     column = jnp.concatenate([jnp.cos(col_angle) * share, jnp.sin(col_angle) * share, lit], 0)
 
-    once[0], offsets, left, column = lax.optimization_barrier((once[0], offsets, left, column))
+    block, left = lax.optimization_barrier((block, left))
+    own.append(block[CUTS[1] :])
+    once.append(shifted(own[1], -1))
+    once[0], offsets, column = lax.optimization_barrier((once[0], offsets, column))
     twice = [shifted(piece, -1) for piece in once]
 
     blocks = own + once + twice[:1]
@@ -289,7 +293,7 @@
     pair = other_core(crosses)
     sides = []
     for a, b in zip(SIDES, SIDES[1:]):
-        both = send[:, a:b].astype(jnp.float32) + pair[0, :, a:b].astype(jnp.float32)
+        both = send[:, a:b].astype(jnp.float32) + pair[: send.shape[0], a:b].astype(jnp.float32)
         sides.append(other_chip(both.astype(jnp.bfloat16)))
 
     spots = None

time: 66.2 us -> 65.8 us (level)
  local copies, waits for them, and re-layouts: 1.29 us -> 3.11 us
  starting transfers between devices: 49.1 us -> 47.3 us
  Pallas kernels: 9.22 us -> 8.49 us
    unnamed x16, local copies, waits for them, and re-layouts: 0.05 us -> 1.9 us
    ppermute x4, starting transfers between devices: 31.7 us -> 30.1 us  [shifted(): lax.ppermute(value, 'tile', [(i, (i + by) % count) for i in range(count)])]
    pallas_call x2, Pallas kernels: 5.27 us -> 4.54 us  [spots_of(): pl.pallas_call(functools.partial(final_kernel, chunks, len(grown)), grid=...]
  transfers between devices with their start and end apart: 9 -> 9, of which waited for: 3 -> 3; matrix products, arithmetic and copies ran while one was open for 3% -> 3% of each run, Pallas kernels for 7% -> 6%
where the time goes in v4:
time: 65.8 us; the launch traced here: 65.4 us
  starting transfers between devices  47.3 us (72%)
  Pallas kernels  8.49 us (13%)
  waiting for transfers between devices  4.2 us (6%)
  local copies, waits for them, and re-layouts  3.11 us (5%)
  other arithmetic  1.97 us (3%)
    ppermute x4, starting transfers between devices, shifted(): lax.ppermute(value, 'tile', [(i, (i + by) % count) for i in range(count)])  30.1 us
    ppermute x3, starting transfers between devices, other_chip(): return lax.ppermute(value, 'dir', [(0, 2), (1, 3), (2, 0), (3, 1)])  11.3 us
    ppermute x2, starting transfers between devices, other_core(): return lax.ppermute(value, 'dir', [(0, 1), (1, 0), (2, 3), (3, 2)])  5.92 us
    pallas_call x2, Pallas kernels, spots_of(): pl.pallas_call(functools.partial(final_kernel, chunks, len(grown)), grid=...  4.54 us
    pallas_call x2, Pallas kernels, terms(): pl.pallas_call(functools.partial(term_kernel, first, rows, depths, len(ca...  3.95 us
    ppermute x3, waiting for transfers between devices, other_chip(): return lax.ppermute(value, 'dir', [(0, 2), (1, 3), (2, 0), (3, 1)])  3.06 us
    unnamed x16, local copies, waits for them, and re-layouts  1.9 us
  transfers between devices with their start and end apart: 9, of which 3 were waited for; matrix products, arithmetic and copies ran while one was open for 3% of the time, Pallas kernels for 6%

profile of v4, /device:TPU:1, one launch (start us, length us, event | category | flops | bytes accessed | tf_op | source)
XLA Modules:
  0.0 65.4 jit_solution(12767650084100505578)
XLA Ops:
  0.0 0.0 copy-start.2
  0.0 0.0 copy-start.3
  0.0 1.0 %slice_bitcast_fusion.refs_0_ = bf16[64,2048]{1,0:T(8,128)(2,1)S(1)} fusion(bf16[1,128,2048]{2,1,0:T(8,128)(2,1)} %param.10), kind=kLoop, calls=%fused_computation.4 | loop fusion | bytes 524288 | tf_op jit(solution)/shard_map/slice | solution.py:251
  1.0 15.2 %collective-permute-start = (bf16[64,2048]{1,0:T(8,128)(2,1)S(1)}, bf16[64,2048]{1,0:T(8,128)(2,1)S(1)}, u32[]{:S(2)}, u32[]{:S(2)}) collective-permute-start(bf16[64,2048]{1,0:T(8,128)(2,1)S(1)} %slice_bitcast_fusion.refs_0_), channel_id=1, source_target_pairs={{0,508},{4,0},{8,4},{12,8},{16,12},{20,16},{24,20},{28,24},{32,28}... | collective-permute-start | bytes 786440 | tf_op jit(solution)/shard_map/ppermute | solution.py:43
  16.2 0.0 copy-start.5
  16.2 0.6 copy-done.5
  16.8 0.1 multiply_cosine_fusion.1
  17.0 0.0 copy-done.2
  17.0 0.0 copy-done.3
  17.0 0.0 copy-start.1
  17.0 0.1 negate_convert_fusion
  17.1 0.9 %copy-done.1 = bf16[1,128,2048]{2,1,0:T(8,128)(2,1)S(1)} copy-done((bf16[1,128,2048]{2,1,0:T(8,128)(2,1)S(1)}, bf16[1,128,2048]{2,1,0:T(8,128)(2,1)}, u32[]{:S(2)}) %copy-start.1) | copy-done | bytes 524312
  18.0 0.0 copy-start.6
  18.0 2.6 %collective-permute-start.1 = (bf16[64,2048]{1,0:T(8,128)(2,1)S(1)}, bf16[64,2048]{1,0:T(8,128)(2,1)S(1)}, u32[]{:S(2)}, u32[]{:S(2)}) collective-permute-start(bf16[64,2048]{1,0:T(8,128)(2,1)S(1)} %slice.23.refs_1_.refs_0_), channel_id=1, source_target_pairs={{0,508},{4,0},{8,4},{12,8},{16,12},{20,16},{24,20},{28,24},{32,28}... | collective-permute-start | bytes 786440 | tf_op jit(solution)/shard_map/ppermute | solution.py:43
  20.7 0.0 copy-done.6
  20.7 0.6 reduce_sum.9
  21.3 0.7 divide_sqrt_fusion
  22.0 0.0 copy-start.7
  22.0 0.3 fusion.1
  22.3 0.3 copy-done.7
  22.6 0.1 broadcast_in_dim.8
  22.7 0.0 copy-start.4
  22.7 0.0 collective-permute-done.refs_2_.refs_1_
  22.8 6.7 %collective-permute-start.2 = (bf16[64,2048]{1,0:T(8,128)(2,1)S(1)}, bf16[64,2048]{1,0:T(8,128)(2,1)S(1)}, u32[]{:S(2)}, u32[]{:S(2)}) collective-permute-start(bf16[64,2048]{1,0:T(8,128)(2,1)S(1)} %collective-permute-done.refs_2_.refs_1_), channel_id=1, source_target_pairs={{0,508},{4,0},{8,4},{12,8},{16,12},{20,16},{24,20},{28,24},{32,28}... | collective-permute-start | bytes 786440 | tf_op jit(solution)/shard_map/ppermute | solution.py:43
  29.5 0.0 copy-done.4
  29.5 0.1 copy.12.offsets_ref
  29.6 0.0 collective-permute-done.1.refs_3_.refs_2_
  29.6 5.6 %collective-permute-start.4 = (bf16[64,2048]{1,0:T(8,128)(2,1)S(1)}, bf16[64,2048]{1,0:T(8,128)(2,1)S(1)}, u32[]{:S(2)}, u32[]{:S(2)}) collective-permute-start(bf16[64,2048]{1,0:T(8,128)(2,1)S(1)} %collective-permute-done.1.refs_3_.refs_2_), channel_id=1, source_target_pairs={{0,508},{4,0},{8,4},{12,8},{16,12},{20,16},{24,20},{28,24},{32,28}... | collective-permute-start | bytes 786440 | tf_op jit(solution)/shard_map/ppermute | solution.py:43
  35.2 0.0 collective-permute-done.2.refs_4_.refs_3_
  35.2 1.9 %terms.2 = (bf16[64,2048]{1,0:T(8,128)(2,1)S(1)}, bf16[64,2048]{1,0:T(8,128)(2,1)S(1)}, bf16[64,2048]{1,0:T(8,128)(2,1)S(1)}, bf16[64,2048]{1,0:T(8,128)(2,1)S(1)}) custom-call(s32[1]{0:T(128)} %bitcast.5.index_ref, s32[4,4,2]{2,1,0:T(4,128)S(1)} %copy.12.offsets_ref, bf16[64,2048]{1,0:T(8,128)(2,1)S(1)} %slice_bitcast_fusion.refs_0_, ...), custom_call_target="tpu_custom_call" | custom-call | flops 1024 | bytes 1024 | tf_op jit(solution)/shard_map/terms/pallas_call | solution.py:138
  37.1 3.6 %collective-permute-start.3 = (bf16[64,2048]{1,0:T(8,128)(2,1)S(1)}, bf16[64,2048]{1,0:T(8,128)(2,1)S(1)}, u32[]{:S(2)}, u32[]{:S(2)}) collective-permute-start(bf16[64,2048]{1,0:T(8,128)(2,1)S(1)} %get-tuple-element.25), channel_id=1, source_target_pairs={{0,1},{1,0},{2,3},{3,2},{4,5},{5,4},{6,7},{7,6},{8,9},{9,8},{10,11... | collective-permute-start | bytes 786440 | tf_op jit(solution)/shard_map/ppermute | solution.py:47
  40.8 0.0 collective-permute-done.4.refs_4_
  40.8 1.1 %collective-permute-done.3 = bf16[64,2048]{1,0:T(8,128)(2,1)S(1)} collective-permute-done((bf16[64,2048]{1,0:T(8,128)(2,1)S(1)}, bf16[64,2048]{1,0:T(8,128)(2,1)S(1)}, u32[]{:S(2)}, u32[]{:S(2)}) %collective-permute-start.3) | collective-permute-done | bytes 262176 | tf_op jit(solution)/shard_map/ppermute | solution.py:47
  41.9 2.0 %terms.3 = (bf16[64,2048]{1,0:T(8,128)(2,1)S(1)}, bf16[64,2048]{1,0:T(8,128)(2,1)S(1)}, bf16[192,2048]{1,0:T(8,128)(2,1)S(1)}) custom-call(s32[1]{0:T(128)} %bitcast.5.index_ref, s32[4,4,2]{2,1,0:T(4,128)S(1)} %copy.12.offsets_ref, bf16[64,2048]{1,0:T(8,128)(2,1)S(1)} %slice.23.refs_1_.refs_0_, bf16[64,2048]{1,0:T(8,128)(2,1)S(1)} %collective-permute-done.refs_2_.refs_1_, ...), custom_call_target="tpu_custom_call" | custom-call | flops 1024 | bytes 1024 | tf_op jit(solution)/shard_map/terms/pallas_call | solution.py:138
  43.9 2.3 %collective-permute-start.5 = (bf16[192,2048]{1,0:T(8,128)(2,1)S(1)}, bf16[192,2048]{1,0:T(8,128)(2,1)S(1)}, u32[]{:S(2)}, u32[]{:S(2)}) collective-permute-start(bf16[192,2048]{1,0:T(8,128)(2,1)S(1)} %get-tuple-element.29), channel_id=1, source_target_pairs={{0,1},{1,0},{2,3},{3,2},{4,5},{5,4},{6,7},{7,6},{8,9},{9,8},{10,11... | collective-permute-start | bytes 2359304 | tf_op jit(solution)/shard_map/ppermute | solution.py:47
  46.2 0.1 add_convert_fusion
  46.3 4.5 %collective-permute-start.6 = (bf16[64,2048]{1,0:T(8,128)(2,1)S(1)}, bf16[64,2048]{1,0:T(8,128)(2,1)S(1)}, u32[]{:S(2)}, u32[]{:S(2)}) collective-permute-start(bf16[64,2048]{1,0:T(8,128)(2,1)S(1)} %add_convert_fusion), channel_id=1, source_target_pairs={{0,2},{1,3},{2,0},{3,1},{4,6},{5,7},{6,4},{7,5},{8,10},{9,11},{10,... | collective-permute-start | bytes 786440 | tf_op jit(solution)/shard_map/ppermute | solution.py:51
  50.9 0.0 collective-permute-done.5.refs_2_
  50.9 0.0 copy-start
  50.9 0.1 add_convert_fusion.1
  50.9 2.2 %collective-permute-start.8 = (bf16[64,1024]{1,0:T(8,128)(2,1)S(1)}, bf16[64,1024]{1,0:T(8,128)(2,1)S(1)}, u32[]{:S(2)}, u32[]{:S(2)}) collective-permute-start(bf16[64,1024]{1,0:T(8,128)(2,1)S(1)} %get-tuple-element.33), channel_id=1, source_target_pairs={{0,2},{1,3},{2,0},{3,1},{4,6},{5,7},{6,4},{7,5},{8,10},{9,11},{10,... | collective-permute-start | bytes 393224 | tf_op jit(solution)/shard_map/ppermute | solution.py:51
  53.2 4.5 %collective-permute-start.7 = (bf16[64,1024]{1,0:T(8,128)(2,1)S(1)}, bf16[64,1024]{1,0:T(8,128)(2,1)S(1)}, u32[]{:S(2)}, u32[]{:S(2)}) collective-permute-start(bf16[64,1024]{1,0:T(8,128)(2,1)S(1)} %get-tuple-element.34), channel_id=1, source_target_pairs={{0,2},{1,3},{2,0},{3,1},{4,6},{5,7},{6,4},{7,5},{8,10},{9,11},{10,... | collective-permute-start | bytes 393224 | tf_op jit(solution)/shard_map/ppermute | solution.py:51
  57.8 0.0 collective-permute-done.6.refs_3_
  57.8 2.5 %collective-permute-done.8.refs_4_ = bf16[64,1024]{1,0:T(8,128)(2,1)S(1)} collective-permute-done((bf16[64,1024]{1,0:T(8,128)(2,1)S(1)}, bf16[64,1024]{1,0:T(8,128)(2,1)S(1)}, u32[]{:S(2)}, u32[]{:S(2)}) %collective-permute-start.8) | collective-permute-done | bytes 131104 | tf_op jit(solution)/shard_map/ppermute | solution.py:51
  60.3 0.0 copy-done
  60.3 2.3 %spots.2.refs_5_ = bf16[128,2048]{1,0:T(8,128)(2,1)} custom-call(bf16[768,256]{1,0:T(8,128)(2,1)S(1)} %bitcast.9, bf16[256,256]{1,0:T(8,128)(2,1)S(1)} %copy-done, f32[7,2048]{1,0:T(8,128)S(1)} %pad_maximum_fusion.column_ref, bf16[64,2048]{1,0:T(8,128)(2,1)S(1)} %get-tuple-element.24.refs_0_, bf16[64,2048]{1,0:T(8,128)(2,1)S(1)} %get-tuple-element.28.refs_1_, ...), custom_call_target="tpu_custom_call" | custom-call | flops 1024 | bytes 1024 | tf_op jit(solution)/shard_map/spots/pallas_call | solution.py:228
  62.6 0.5 collective-permute-done.7.refs_4_
  63.1 2.3 %spots.3 = bf16[128,2048]{1,0:T(8,128)(2,1)} custom-call(bf16[768,256]{1,0:T(8,128)(2,1)S(1)} %bitcast.10, bf16[256,256]{1,0:T(8,128)(2,1)S(1)} %copy-done, f32[7,2048]{1,0:T(8,128)S(1)} %pad_maximum_fusion.column_ref, bf16[64,2048]{1,0:T(8,128)(2,1)S(1)} %get-tuple-element.24.refs_0_, ...), custom_call_target="tpu_custom_call", output_to_operand_aliasing={{}: (8, {})} | custom-call | flops 1024 | bytes 1024 | tf_op jit(solution)/shard_map/spots/pallas_call | solution.py:228
  (6 shorter events, 0.1 us)
Async XLA Ops:
  0.0 17.0 %copy-start.2 = (f32[128,128]{1,0:T(8,128)S(1)}, f32[128,128]{1,0:T(8,128)}, u32[]{:S(2)}) copy-start(f32[128,128]{1,0:T(8,128)} %constant.36) | copy-start | bytes 196612
  0.0 17.0 %copy-start.3 = (f32[128,128]{1,0:T(8,128)S(1)}, f32[128,128]{1,0:T(8,128)}, u32[]{:S(2)}) copy-start(f32[128,128]{1,0:T(8,128)} %constant.35) | copy-start | bytes 196612
  1.0 21.7 %collective-permute-start = (bf16[64,2048]{1,0:T(8,128)(2,1)S(1)}, bf16[64,2048]{1,0:T(8,128)(2,1)S(1)}, u32[]{:S(2)}, u32[]{:S(2)}) collective-permute-start(bf16[64,2048]{1,0:T(8,128)(2,1)S(1)} %slice_bitcast_fusion.refs_0_), channel_id=1, source_target_pairs={{0,508},{4,0},{8,4},{12,8},{16,12},{20,16},{24,20},{28,24},{32,28}... | collective-permute-start | bytes 786440 | tf_op jit(solution)/shard_map/ppermute | solution.py:43
  16.2 0.7 %copy-start.5 = (f32[3]{0:T(128)S(1)}, f32[3]{0:T(128)}, u32[]{:S(2)}) copy-start(f32[3]{0:T(128)} %param.13) | copy-start | bytes 40
  17.0 1.0 %copy-start.1 = (bf16[1,128,2048]{2,1,0:T(8,128)(2,1)S(1)}, bf16[1,128,2048]{2,1,0:T(8,128)(2,1)}, u32[]{:S(2)}) copy-start(bf16[1,128,2048]{2,1,0:T(8,128)(2,1)} %param.10) | copy-start | bytes 1572868
  18.0 2.7 %copy-start.6 = (f32[3]{0:T(128)S(1)}, f32[3]{0:T(128)}, u32[]{:S(2)}) copy-start(f32[3]{0:T(128)} %param.14) | copy-start | bytes 40
  18.0 11.5 %collective-permute-start.1 = (bf16[64,2048]{1,0:T(8,128)(2,1)S(1)}, bf16[64,2048]{1,0:T(8,128)(2,1)S(1)}, u32[]{:S(2)}, u32[]{:S(2)}) collective-permute-start(bf16[64,2048]{1,0:T(8,128)(2,1)S(1)} %slice.23.refs_1_.refs_0_), channel_id=1, source_target_pairs={{0,508},{4,0},{8,4},{12,8},{16,12},{20,16},{24,20},{28,24},{32,28}... | collective-permute-start | bytes 786440 | tf_op jit(solution)/shard_map/ppermute | solution.py:43
  22.0 0.7 %copy-start.7 = (s32[1,16]{1,0:T(1,128)S(1)}, s32[1,16]{1,0:T(1,128)}, u32[]{:S(2)}) copy-start(s32[1,16]{1,0:T(1,128)} %param.12) | copy-start | bytes 196
  22.7 6.7 %copy-start.4 = (s32[4,4,2]{1,2,0:T(2,128)S(1)}, s32[4,4,2]{1,2,0:T(2,128)}, u32[]{:S(2)}) copy-start(s32[4,4,2]{1,2,0:T(2,128)} %param.11) | copy-start | bytes 388
  22.8 12.4 %collective-permute-start.2 = (bf16[64,2048]{1,0:T(8,128)(2,1)S(1)}, bf16[64,2048]{1,0:T(8,128)(2,1)S(1)}, u32[]{:S(2)}, u32[]{:S(2)}) collective-permute-start(bf16[64,2048]{1,0:T(8,128)(2,1)S(1)} %collective-permute-done.refs_2_.refs_1_), channel_id=1, source_target_pairs={{0,508},{4,0},{8,4},{12,8},{16,12},{20,16},{24,20},{28,24},{32,28}... | collective-permute-start | bytes 786440 | tf_op jit(solution)/shard_map/ppermute | solution.py:43
  29.6 11.2 %collective-permute-start.4 = (bf16[64,2048]{1,0:T(8,128)(2,1)S(1)}, bf16[64,2048]{1,0:T(8,128)(2,1)S(1)}, u32[]{:S(2)}, u32[]{:S(2)}) collective-permute-start(bf16[64,2048]{1,0:T(8,128)(2,1)S(1)} %collective-permute-done.1.refs_3_.refs_2_), channel_id=1, source_target_pairs={{0,508},{4,0},{8,4},{12,8},{16,12},{20,16},{24,20},{28,24},{32,28}... | collective-permute-start | bytes 786440 | tf_op jit(solution)/shard_map/ppermute | solution.py:43
  37.1 4.8 %collective-permute-start.3 = (bf16[64,2048]{1,0:T(8,128)(2,1)S(1)}, bf16[64,2048]{1,0:T(8,128)(2,1)S(1)}, u32[]{:S(2)}, u32[]{:S(2)}) collective-permute-start(bf16[64,2048]{1,0:T(8,128)(2,1)S(1)} %get-tuple-element.25), channel_id=1, source_target_pairs={{0,1},{1,0},{2,3},{3,2},{4,5},{5,4},{6,7},{7,6},{8,9},{9,8},{10,11... | collective-permute-start | bytes 786440 | tf_op jit(solution)/shard_map/ppermute | solution.py:47
  43.9 6.9 %collective-permute-start.5 = (bf16[192,2048]{1,0:T(8,128)(2,1)S(1)}, bf16[192,2048]{1,0:T(8,128)(2,1)S(1)}, u32[]{:S(2)}, u32[]{:S(2)}) collective-permute-start(bf16[192,2048]{1,0:T(8,128)(2,1)S(1)} %get-tuple-element.29), channel_id=1, source_target_pairs={{0,1},{1,0},{2,3},{3,2},{4,5},{5,4},{6,7},{7,6},{8,9},{9,8},{10,11... | collective-permute-start | bytes 2359304 | tf_op jit(solution)/shard_map/ppermute | solution.py:47
  46.3 11.5 %collective-permute-start.6 = (bf16[64,2048]{1,0:T(8,128)(2,1)S(1)}, bf16[64,2048]{1,0:T(8,128)(2,1)S(1)}, u32[]{:S(2)}, u32[]{:S(2)}) collective-permute-start(bf16[64,2048]{1,0:T(8,128)(2,1)S(1)} %add_convert_fusion), channel_id=1, source_target_pairs={{0,2},{1,3},{2,0},{3,1},{4,6},{5,7},{6,4},{7,5},{8,10},{9,11},{10,... | collective-permute-start | bytes 786440 | tf_op jit(solution)/shard_map/ppermute | solution.py:51
  50.9 9.4 %copy-start = (bf16[256,256]{1,0:T(8,128)(2,1)S(1)}, bf16[256,256]{1,0:T(8,128)(2,1)}, u32[]{:S(2)}) copy-start(bf16[256,256]{1,0:T(8,128)(2,1)} %constant.32.clone.right_ref) | copy-start | bytes 393220
  50.9 9.3 %collective-permute-start.8 = (bf16[64,1024]{1,0:T(8,128)(2,1)S(1)}, bf16[64,1024]{1,0:T(8,128)(2,1)S(1)}, u32[]{:S(2)}, u32[]{:S(2)}) collective-permute-start(bf16[64,1024]{1,0:T(8,128)(2,1)S(1)} %get-tuple-element.33), channel_id=1, source_target_pairs={{0,2},{1,3},{2,0},{3,1},{4,6},{5,7},{6,4},{7,5},{8,10},{9,11},{10,... | collective-permute-start | bytes 393224 | tf_op jit(solution)/shard_map/ppermute | solution.py:51
  53.2 9.9 %collective-permute-start.7 = (bf16[64,1024]{1,0:T(8,128)(2,1)S(1)}, bf16[64,1024]{1,0:T(8,128)(2,1)S(1)}, u32[]{:S(2)}, u32[]{:S(2)}) collective-permute-start(bf16[64,1024]{1,0:T(8,128)(2,1)S(1)} %get-tuple-element.34), channel_id=1, source_target_pairs={{0,2},{1,3},{2,0},{3,1},{4,6},{5,7},{6,4},{7,5},{8,10},{9,11},{10,... | collective-permute-start | bytes 393224 | tf_op jit(solution)/shard_map/ppermute | solution.py:51

commit v5 on v4

--- a/solution.py
+++ b/solution.py
@@ -274,10 +274,10 @@
     lit = jnp.repeat(subap_valid.astype(jnp.float32), SUBPIX, axis=1)
     column = jnp.concatenate([jnp.cos(col_angle) * share, jnp.sin(col_angle) * share, lit], 0)
 
-    block, left = lax.optimization_barrier((block, left))
+    block = lax.optimization_barrier(block)
     own.append(block[CUTS[1] :])
     once.append(shifted(own[1], -1))
-    once[0], offsets, column = lax.optimization_barrier((once[0], offsets, column))
+    once[0], offsets, column, left = lax.optimization_barrier((once[0], offsets, column, left))
     twice = [shifted(piece, -1) for piece in once]
 
     blocks = own + once + twice[:1]

time: 65.8 us -> 65.8 us (level)
  local copies, waits for them, and re-layouts: 3.11 us -> 1.29 us
  starting transfers between devices: 47.3 us -> 49.1 us
    unnamed x16, local copies, waits for them, and re-layouts: 1.9 us -> 0.05 us
    ppermute x4, starting transfers between devices: 30.1 us -> 31.7 us  [shifted(): lax.ppermute(value, 'tile', [(i, (i + by) % count) for i in range(count)])]
where the time goes in v5:
time: 65.8 us; the launch traced here: 65.4 us
  starting transfers between devices  49.1 us (75%)
  Pallas kernels  8.48 us (13%)
  waiting for transfers between devices  4.24 us (6%)
  other arithmetic  1.97 us (3%)
  local copies, waits for them, and re-layouts  1.29 us (2%)
    ppermute x4, starting transfers between devices, shifted(): lax.ppermute(value, 'tile', [(i, (i + by) % count) for i in range(count)])  31.7 us
    ppermute x3, starting transfers between devices, other_chip(): return lax.ppermute(value, 'dir', [(0, 2), (1, 3), (2, 0), (3, 1)])  11.3 us
    ppermute x2, starting transfers between devices, other_core(): return lax.ppermute(value, 'dir', [(0, 1), (1, 0), (2, 3), (3, 2)])  6.02 us
    pallas_call x2, Pallas kernels, spots_of(): pl.pallas_call(functools.partial(final_kernel, chunks, len(grown)), grid=...  4.54 us
    pallas_call x2, Pallas kernels, terms(): pl.pallas_call(functools.partial(term_kernel, first, rows, depths, len(ca...  3.94 us
    ppermute x3, waiting for transfers between devices, other_chip(): return lax.ppermute(value, 'dir', [(0, 2), (1, 3), (2, 0), (3, 1)])  3.05 us
  transfers between devices with their start and end apart: 9, of which 3 were waited for; matrix products, arithmetic and copies ran while one was open for 3% of the time, Pallas kernels for 6%

profile of v5, /device:TPU:1, one launch (start us, length us, event | category | flops | bytes accessed | tf_op | source)
XLA Modules:
  0.0 65.4 jit_solution(3378428012751070774)
XLA Ops:
  0.0 0.0 copy-start.1
  0.0 1.0 %slice_bitcast_fusion.refs_0_ = bf16[64,2048]{1,0:T(8,128)(2,1)S(1)} fusion(bf16[1,128,2048]{2,1,0:T(8,128)(2,1)} %param.10), kind=kLoop, calls=%fused_computation.4 | loop fusion | bytes 524288 | tf_op jit(solution)/shard_map/slice | solution.py:251
  1.0 15.2 %collective-permute-start = (bf16[64,2048]{1,0:T(8,128)(2,1)S(1)}, bf16[64,2048]{1,0:T(8,128)(2,1)S(1)}, u32[]{:S(2)}, u32[]{:S(2)}) collective-permute-start(bf16[64,2048]{1,0:T(8,128)(2,1)S(1)} %slice_bitcast_fusion.refs_0_), channel_id=1, source_target_pairs={{0,508},{4,0},{8,4},{12,8},{16,12},{20,16},{24,20},{28,24},{32,28}... | collective-permute-start | bytes 786440 | tf_op jit(solution)/shard_map/ppermute | solution.py:43
  16.2 0.0 copy-done.1
  16.2 0.0 copy-start.6
  16.2 0.0 copy-start.7
  16.2 0.0 copy-start.5
  16.3 0.0 copy-start.3
  16.3 0.0 copy-start.2
  16.3 2.8 %collective-permute-start.1 = (bf16[64,2048]{1,0:T(8,128)(2,1)S(1)}, bf16[64,2048]{1,0:T(8,128)(2,1)S(1)}, u32[]{:S(2)}, u32[]{:S(2)}) collective-permute-start(bf16[64,2048]{1,0:T(8,128)(2,1)S(1)} %slice.28.refs_1_.refs_0_), channel_id=1, source_target_pairs={{0,508},{4,0},{8,4},{12,8},{16,12},{20,16},{24,20},{28,24},{32,28}... | collective-permute-start | bytes 786440 | tf_op jit(solution)/shard_map/ppermute | solution.py:43
  19.1 0.0 copy-done.6
  19.1 0.6 reduce_sum.9
  19.7 0.7 divide_sqrt_fusion
  20.4 0.0 copy-done.7
  20.4 0.0 copy-done.5
  20.4 0.1 multiply_cosine_fusion.1
  20.5 0.3 fusion.1
  20.9 0.0 copy-done.3
  20.9 0.0 copy-done.2
  20.9 0.1 negate_convert_fusion
  21.0 0.1 broadcast_in_dim.8
  21.1 0.0 copy-start.4
  21.1 0.0 collective-permute-done.refs_2_.refs_1_
  21.2 8.3 %collective-permute-start.2 = (bf16[64,2048]{1,0:T(8,128)(2,1)S(1)}, bf16[64,2048]{1,0:T(8,128)(2,1)S(1)}, u32[]{:S(2)}, u32[]{:S(2)}) collective-permute-start(bf16[64,2048]{1,0:T(8,128)(2,1)S(1)} %collective-permute-done.refs_2_.refs_1_), channel_id=1, source_target_pairs={{0,508},{4,0},{8,4},{12,8},{16,12},{20,16},{24,20},{28,24},{32,28}... | collective-permute-start | bytes 786440 | tf_op jit(solution)/shard_map/ppermute | solution.py:43
  29.5 0.0 copy-done.4
  29.5 0.1 copy.12.offsets_ref
  29.6 0.0 collective-permute-done.1.refs_3_.refs_2_
  29.6 5.5 %collective-permute-start.4 = (bf16[64,2048]{1,0:T(8,128)(2,1)S(1)}, bf16[64,2048]{1,0:T(8,128)(2,1)S(1)}, u32[]{:S(2)}, u32[]{:S(2)}) collective-permute-start(bf16[64,2048]{1,0:T(8,128)(2,1)S(1)} %collective-permute-done.1.refs_3_.refs_2_), channel_id=1, source_target_pairs={{0,508},{4,0},{8,4},{12,8},{16,12},{20,16},{24,20},{28,24},{32,28}... | collective-permute-start | bytes 786440 | tf_op jit(solution)/shard_map/ppermute | solution.py:43
  35.1 0.0 collective-permute-done.2.refs_4_.refs_3_
  35.1 1.9 %terms.2 = (bf16[64,2048]{1,0:T(8,128)(2,1)S(1)}, bf16[64,2048]{1,0:T(8,128)(2,1)S(1)}, bf16[64,2048]{1,0:T(8,128)(2,1)S(1)}, bf16[64,2048]{1,0:T(8,128)(2,1)S(1)}) custom-call(s32[1]{0:T(128)} %bitcast.4.index_ref, s32[4,4,2]{2,1,0:T(4,128)S(1)} %copy.12.offsets_ref, bf16[64,2048]{1,0:T(8,128)(2,1)S(1)} %slice_bitcast_fusion.refs_0_, ...), custom_call_target="tpu_custom_call" | custom-call | flops 1024 | bytes 1024 | tf_op jit(solution)/shard_map/terms/pallas_call | solution.py:138
  37.1 3.7 %collective-permute-start.3 = (bf16[64,2048]{1,0:T(8,128)(2,1)S(1)}, bf16[64,2048]{1,0:T(8,128)(2,1)S(1)}, u32[]{:S(2)}, u32[]{:S(2)}) collective-permute-start(bf16[64,2048]{1,0:T(8,128)(2,1)S(1)} %get-tuple-element.23), channel_id=1, source_target_pairs={{0,1},{1,0},{2,3},{3,2},{4,5},{5,4},{6,7},{7,6},{8,9},{9,8},{10,11... | collective-permute-start | bytes 786440 | tf_op jit(solution)/shard_map/ppermute | solution.py:47
  40.8 0.0 collective-permute-done.4.refs_4_
  40.8 1.1 %collective-permute-done.3 = bf16[64,2048]{1,0:T(8,128)(2,1)S(1)} collective-permute-done((bf16[64,2048]{1,0:T(8,128)(2,1)S(1)}, bf16[64,2048]{1,0:T(8,128)(2,1)S(1)}, u32[]{:S(2)}, u32[]{:S(2)}) %collective-permute-start.3) | collective-permute-done | bytes 262176 | tf_op jit(solution)/shard_map/ppermute | solution.py:47
  42.0 2.0 %terms.3 = (bf16[64,2048]{1,0:T(8,128)(2,1)S(1)}, bf16[64,2048]{1,0:T(8,128)(2,1)S(1)}, bf16[192,2048]{1,0:T(8,128)(2,1)S(1)}) custom-call(s32[1]{0:T(128)} %bitcast.4.index_ref, s32[4,4,2]{2,1,0:T(4,128)S(1)} %copy.12.offsets_ref, bf16[64,2048]{1,0:T(8,128)(2,1)S(1)} %slice.28.refs_1_.refs_0_, bf16[64,2048]{1,0:T(8,128)(2,1)S(1)} %collective-permute-done.refs_2_.refs_1_, ...), custom_call_target="tpu_custom_call" | custom-call | flops 1024 | bytes 1024 | tf_op jit(solution)/shard_map/terms/pallas_call | solution.py:138
  44.0 2.3 %collective-permute-start.5 = (bf16[192,2048]{1,0:T(8,128)(2,1)S(1)}, bf16[192,2048]{1,0:T(8,128)(2,1)S(1)}, u32[]{:S(2)}, u32[]{:S(2)}) collective-permute-start(bf16[192,2048]{1,0:T(8,128)(2,1)S(1)} %get-tuple-element.27), channel_id=1, source_target_pairs={{0,1},{1,0},{2,3},{3,2},{4,5},{5,4},{6,7},{7,6},{8,9},{9,8},{10,11... | collective-permute-start | bytes 2359304 | tf_op jit(solution)/shard_map/ppermute | solution.py:47
  46.2 0.1 add_convert_fusion
  46.3 4.5 %collective-permute-start.6 = (bf16[64,2048]{1,0:T(8,128)(2,1)S(1)}, bf16[64,2048]{1,0:T(8,128)(2,1)S(1)}, u32[]{:S(2)}, u32[]{:S(2)}) collective-permute-start(bf16[64,2048]{1,0:T(8,128)(2,1)S(1)} %add_convert_fusion), channel_id=1, source_target_pairs={{0,2},{1,3},{2,0},{3,1},{4,6},{5,7},{6,4},{7,5},{8,10},{9,11},{10,... | collective-permute-start | bytes 786440 | tf_op jit(solution)/shard_map/ppermute | solution.py:51
  50.9 0.0 collective-permute-done.5.refs_2_
  50.9 0.0 copy-start
  50.9 0.1 add_convert_fusion.1
  51.0 2.2 %collective-permute-start.8 = (bf16[64,1024]{1,0:T(8,128)(2,1)S(1)}, bf16[64,1024]{1,0:T(8,128)(2,1)S(1)}, u32[]{:S(2)}, u32[]{:S(2)}) collective-permute-start(bf16[64,1024]{1,0:T(8,128)(2,1)S(1)} %get-tuple-element.31), channel_id=1, source_target_pairs={{0,2},{1,3},{2,0},{3,1},{4,6},{5,7},{6,4},{7,5},{8,10},{9,11},{10,... | collective-permute-start | bytes 393224 | tf_op jit(solution)/shard_map/ppermute | solution.py:51
  53.2 4.5 %collective-permute-start.7 = (bf16[64,1024]{1,0:T(8,128)(2,1)S(1)}, bf16[64,1024]{1,0:T(8,128)(2,1)S(1)}, u32[]{:S(2)}, u32[]{:S(2)}) collective-permute-start(bf16[64,1024]{1,0:T(8,128)(2,1)S(1)} %get-tuple-element.32), channel_id=1, source_target_pairs={{0,2},{1,3},{2,0},{3,1},{4,6},{5,7},{6,4},{7,5},{8,10},{9,11},{10,... | collective-permute-start | bytes 393224 | tf_op jit(solution)/shard_map/ppermute | solution.py:51
  57.8 0.0 collective-permute-done.6.refs_3_
  57.8 2.5 %collective-permute-done.8.refs_4_ = bf16[64,1024]{1,0:T(8,128)(2,1)S(1)} collective-permute-done((bf16[64,1024]{1,0:T(8,128)(2,1)S(1)}, bf16[64,1024]{1,0:T(8,128)(2,1)S(1)}, u32[]{:S(2)}, u32[]{:S(2)}) %collective-permute-start.8) | collective-permute-done | bytes 131104 | tf_op jit(solution)/shard_map/ppermute | solution.py:51
  60.3 0.0 copy-done
  60.3 2.3 %spots.2.refs_5_ = bf16[128,2048]{1,0:T(8,128)(2,1)} custom-call(bf16[768,256]{1,0:T(8,128)(2,1)S(1)} %bitcast.9, bf16[256,256]{1,0:T(8,128)(2,1)S(1)} %copy-done, f32[7,2048]{1,0:T(8,128)S(1)} %pad_maximum_fusion.column_ref, bf16[64,2048]{1,0:T(8,128)(2,1)S(1)} %get-tuple-element.22.refs_0_, bf16[64,2048]{1,0:T(8,128)(2,1)S(1)} %get-tuple-element.26.refs_1_, ...), custom_call_target="tpu_custom_call" | custom-call | flops 1024 | bytes 1024 | tf_op jit(solution)/shard_map/spots/pallas_call | solution.py:228
  62.6 0.5 collective-permute-done.7.refs_4_
  63.1 2.3 %spots.3 = bf16[128,2048]{1,0:T(8,128)(2,1)} custom-call(bf16[768,256]{1,0:T(8,128)(2,1)S(1)} %bitcast.10, bf16[256,256]{1,0:T(8,128)(2,1)S(1)} %copy-done, f32[7,2048]{1,0:T(8,128)S(1)} %pad_maximum_fusion.column_ref, bf16[64,2048]{1,0:T(8,128)(2,1)S(1)} %get-tuple-element.22.refs_0_, ...), custom_call_target="tpu_custom_call", output_to_operand_aliasing={{}: (8, {})} | custom-call | flops 1024 | bytes 1024 | tf_op jit(solution)/shard_map/spots/pallas_call | solution.py:228
  (6 shorter events, 0.1 us)
Async XLA Ops:
  0.0 16.2 %copy-start.1 = (bf16[1,128,2048]{2,1,0:T(8,128)(2,1)S(1)}, bf16[1,128,2048]{2,1,0:T(8,128)(2,1)}, u32[]{:S(2)}) copy-start(bf16[1,128,2048]{2,1,0:T(8,128)(2,1)} %param.10) | copy-start | bytes 1572868
  1.0 20.1 %collective-permute-start = (bf16[64,2048]{1,0:T(8,128)(2,1)S(1)}, bf16[64,2048]{1,0:T(8,128)(2,1)S(1)}, u32[]{:S(2)}, u32[]{:S(2)}) collective-permute-start(bf16[64,2048]{1,0:T(8,128)(2,1)S(1)} %slice_bitcast_fusion.refs_0_), channel_id=1, source_target_pairs={{0,508},{4,0},{8,4},{12,8},{16,12},{20,16},{24,20},{28,24},{32,28}... | collective-permute-start | bytes 786440 | tf_op jit(solution)/shard_map/ppermute | solution.py:43
  16.2 2.9 %copy-start.6 = (f32[3]{0:T(128)S(1)}, f32[3]{0:T(128)}, u32[]{:S(2)}) copy-start(f32[3]{0:T(128)} %param.14) | copy-start | bytes 40
  16.2 4.2 %copy-start.7 = (s32[1,16]{1,0:T(1,128)S(1)}, s32[1,16]{1,0:T(1,128)}, u32[]{:S(2)}) copy-start(s32[1,16]{1,0:T(1,128)} %param.12) | copy-start | bytes 196
  16.2 4.2 %copy-start.5 = (f32[3]{0:T(128)S(1)}, f32[3]{0:T(128)}, u32[]{:S(2)}) copy-start(f32[3]{0:T(128)} %param.13) | copy-start | bytes 40
  16.3 4.6 %copy-start.3 = (f32[128,128]{1,0:T(8,128)S(1)}, f32[128,128]{1,0:T(8,128)}, u32[]{:S(2)}) copy-start(f32[128,128]{1,0:T(8,128)} %constant.35) | copy-start | bytes 196612
  16.3 4.6 %copy-start.2 = (f32[128,128]{1,0:T(8,128)S(1)}, f32[128,128]{1,0:T(8,128)}, u32[]{:S(2)}) copy-start(f32[128,128]{1,0:T(8,128)} %constant.36) | copy-start | bytes 196612
  16.3 13.3 %collective-permute-start.1 = (bf16[64,2048]{1,0:T(8,128)(2,1)S(1)}, bf16[64,2048]{1,0:T(8,128)(2,1)S(1)}, u32[]{:S(2)}, u32[]{:S(2)}) collective-permute-start(bf16[64,2048]{1,0:T(8,128)(2,1)S(1)} %slice.28.refs_1_.refs_0_), channel_id=1, source_target_pairs={{0,508},{4,0},{8,4},{12,8},{16,12},{20,16},{24,20},{28,24},{32,28}... | collective-permute-start | bytes 786440 | tf_op jit(solution)/shard_map/ppermute | solution.py:43
  21.1 8.4 %copy-start.4 = (s32[4,4,2]{1,2,0:T(2,128)S(1)}, s32[4,4,2]{1,2,0:T(2,128)}, u32[]{:S(2)}) copy-start(s32[4,4,2]{1,2,0:T(2,128)} %param.11) | copy-start | bytes 388
  21.2 13.9 %collective-permute-start.2 = (bf16[64,2048]{1,0:T(8,128)(2,1)S(1)}, bf16[64,2048]{1,0:T(8,128)(2,1)S(1)}, u32[]{:S(2)}, u32[]{:S(2)}) collective-permute-start(bf16[64,2048]{1,0:T(8,128)(2,1)S(1)} %collective-permute-done.refs_2_.refs_1_), channel_id=1, source_target_pairs={{0,508},{4,0},{8,4},{12,8},{16,12},{20,16},{24,20},{28,24},{32,28}... | collective-permute-start | bytes 786440 | tf_op jit(solution)/shard_map/ppermute | solution.py:43
  29.6 11.2 %collective-permute-start.4 = (bf16[64,2048]{1,0:T(8,128)(2,1)S(1)}, bf16[64,2048]{1,0:T(8,128)(2,1)S(1)}, u32[]{:S(2)}, u32[]{:S(2)}) collective-permute-start(bf16[64,2048]{1,0:T(8,128)(2,1)S(1)} %collective-permute-done.1.refs_3_.refs_2_), channel_id=1, source_target_pairs={{0,508},{4,0},{8,4},{12,8},{16,12},{20,16},{24,20},{28,24},{32,28}... | collective-permute-start | bytes 786440 | tf_op jit(solution)/shard_map/ppermute | solution.py:43
  37.1 4.9 %collective-permute-start.3 = (bf16[64,2048]{1,0:T(8,128)(2,1)S(1)}, bf16[64,2048]{1,0:T(8,128)(2,1)S(1)}, u32[]{:S(2)}, u32[]{:S(2)}) collective-permute-start(bf16[64,2048]{1,0:T(8,128)(2,1)S(1)} %get-tuple-element.23), channel_id=1, source_target_pairs={{0,1},{1,0},{2,3},{3,2},{4,5},{5,4},{6,7},{7,6},{8,9},{9,8},{10,11... | collective-permute-start | bytes 786440 | tf_op jit(solution)/shard_map/ppermute | solution.py:47
  44.0 6.9 %collective-permute-start.5 = (bf16[192,2048]{1,0:T(8,128)(2,1)S(1)}, bf16[192,2048]{1,0:T(8,128)(2,1)S(1)}, u32[]{:S(2)}, u32[]{:S(2)}) collective-permute-start(bf16[192,2048]{1,0:T(8,128)(2,1)S(1)} %get-tuple-element.27), channel_id=1, source_target_pairs={{0,1},{1,0},{2,3},{3,2},{4,5},{5,4},{6,7},{7,6},{8,9},{9,8},{10,11... | collective-permute-start | bytes 2359304 | tf_op jit(solution)/shard_map/ppermute | solution.py:47
  46.3 11.5 %collective-permute-start.6 = (bf16[64,2048]{1,0:T(8,128)(2,1)S(1)}, bf16[64,2048]{1,0:T(8,128)(2,1)S(1)}, u32[]{:S(2)}, u32[]{:S(2)}) collective-permute-start(bf16[64,2048]{1,0:T(8,128)(2,1)S(1)} %add_convert_fusion), channel_id=1, source_target_pairs={{0,2},{1,3},{2,0},{3,1},{4,6},{5,7},{6,4},{7,5},{8,10},{9,11},{10,... | collective-permute-start | bytes 786440 | tf_op jit(solution)/shard_map/ppermute | solution.py:51
  50.9 9.4 %copy-start = (bf16[256,256]{1,0:T(8,128)(2,1)S(1)}, bf16[256,256]{1,0:T(8,128)(2,1)}, u32[]{:S(2)}) copy-start(bf16[256,256]{1,0:T(8,128)(2,1)} %constant.32.clone.right_ref) | copy-start | bytes 393220
  51.0 9.3 %collective-permute-start.8 = (bf16[64,1024]{1,0:T(8,128)(2,1)S(1)}, bf16[64,1024]{1,0:T(8,128)(2,1)S(1)}, u32[]{:S(2)}, u32[]{:S(2)}) collective-permute-start(bf16[64,1024]{1,0:T(8,128)(2,1)S(1)} %get-tuple-element.31), channel_id=1, source_target_pairs={{0,2},{1,3},{2,0},{3,1},{4,6},{5,7},{6,4},{7,5},{8,10},{9,11},{10,... | collective-permute-start | bytes 393224 | tf_op jit(solution)/shard_map/ppermute | solution.py:51
  53.2 9.9 %collective-permute-start.7 = (bf16[64,1024]{1,0:T(8,128)(2,1)S(1)}, bf16[64,1024]{1,0:T(8,128)(2,1)S(1)}, u32[]{:S(2)}, u32[]{:S(2)}) collective-permute-start(bf16[64,1024]{1,0:T(8,128)(2,1)S(1)} %get-tuple-element.32), channel_id=1, source_target_pairs={{0,2},{1,3},{2,0},{3,1},{4,6},{5,7},{6,4},{7,5},{8,10},{9,11},{10,... | collective-permute-start | bytes 393224 | tf_op jit(solution)/shard_map/ppermute | solution.py:51

commit v6 on v5

--- a/solution.py
+++ b/solution.py
@@ -18,7 +18,7 @@
 PCOLS = 2048
 DIRS = 4
 
-CUTS = (0, 64, 128)
+CUTS = (0, 48, 128)
 SIDES = (0, 1024, 2048)
 FINAL_COLS = 1024
 LANES = 128

time: 65.8 us -> 66.9 us (1.017)
  local copies, waits for them, and re-layouts: 1.29 us -> 2.2 us
    slice x1, local copies, waits for them, and re-layouts: 0.02 us -> 1.03 us  [shards(): own.append(block[CUTS[1]:])]
    ppermute x2, starting transfers between devices: 6.02 us -> 6.97 us  [other_core(): return lax.ppermute(value, 'dir', [(0, 1), (1, 0), (2, 3), (3, 2)])]
    ppermute x4, starting transfers between devices: 31.7 us -> 30.9 us  [shifted(): lax.ppermute(value, 'tile', [(i, (i + by) % count) for i in range(count)])]
  transfers between devices with their start and end apart: 9 -> 9, of which waited for: 3 -> 3; matrix products, arithmetic and copies ran while one was open for 3% -> 5% of each run, Pallas kernels for 6% -> 6%
where the time goes in v6:
time: 66.9 us; the launch traced here: 66.4 us
  starting transfers between devices  49.2 us (74%)
  Pallas kernels  8.37 us (13%)
  waiting for transfers between devices  4.39 us (7%)
  local copies, waits for them, and re-layouts  2.2 us (3%)
  other arithmetic  1.99 us (3%)
    ppermute x4, starting transfers between devices, shifted(): lax.ppermute(value, 'tile', [(i, (i + by) % count) for i in range(count)])  30.9 us
    ppermute x3, starting transfers between devices, other_chip(): return lax.ppermute(value, 'dir', [(0, 2), (1, 3), (2, 0), (3, 1)])  11.3 us
    ppermute x2, starting transfers between devices, other_core(): return lax.ppermute(value, 'dir', [(0, 1), (1, 0), (2, 3), (3, 2)])  6.97 us
    pallas_call x2, Pallas kernels, spots_of(): pl.pallas_call(functools.partial(final_kernel, chunks, len(grown)), grid=...  4.54 us
    pallas_call x2, Pallas kernels, terms(): pl.pallas_call(functools.partial(term_kernel, first, rows, depths, len(ca...  3.83 us
    ppermute x3, waiting for transfers between devices, other_chip(): return lax.ppermute(value, 'dir', [(0, 2), (1, 3), (2, 0), (3, 1)])  3.32 us
  transfers between devices with their start and end apart: 9, of which 3 were waited for; matrix products, arithmetic and copies ran while one was open for 5% of the time, Pallas kernels for 6%

profile of v6, /device:TPU:1, one launch (start us, length us, event | category | flops | bytes accessed | tf_op | source)
XLA Modules:
  0.0 66.4 jit_solution(13178782304791587601)
XLA Ops:
  0.0 0.9 %slice_bitcast_fusion.refs_0_ = bf16[48,2048]{1,0:T(8,128)(2,1)S(1)} fusion(bf16[1,128,2048]{2,1,0:T(8,128)(2,1)} %param.10), kind=kLoop, calls=%fused_computation.8 | loop fusion | bytes 393216 | tf_op jit(solution)/shard_map/slice | solution.py:251
  0.9 15.2 %collective-permute-start = (bf16[48,2048]{1,0:T(8,128)(2,1)S(1)}, bf16[48,2048]{1,0:T(8,128)(2,1)S(1)}, u32[]{:S(2)}, u32[]{:S(2)}) collective-permute-start(bf16[48,2048]{1,0:T(8,128)(2,1)S(1)} %slice_bitcast_fusion.refs_0_), channel_id=1, source_target_pairs={{0,508},{4,0},{8,4},{12,8},{16,12},{20,16},{24,20},{28,24},{32,28}... | collective-permute-start | bytes 589832 | tf_op jit(solution)/shard_map/ppermute | solution.py:43
  16.1 0.0 copy-start.5
  16.1 0.0 copy-start.6
  16.1 0.0 copy-start.4
  16.1 0.0 copy-start.2
  16.2 1.0 %slice.28.refs_1_.refs_0_ = bf16[80,2048]{1,0:T(8,128)(2,1)S(1)} slice(bf16[128,2048]{1,0:T(8,128)(2,1)} %bitcast.11), slice={[48:128], [0:2048]} | slice | bytes 655360 | tf_op jit(solution)/shard_map/slice | solution.py:278
  17.2 0.0 copy-start.1
  17.2 2.8 %collective-permute-start.1 = (bf16[80,2048]{1,0:T(8,128)(2,1)S(1)}, bf16[80,2048]{1,0:T(8,128)(2,1)S(1)}, u32[]{:S(2)}, u32[]{:S(2)}) collective-permute-start(bf16[80,2048]{1,0:T(8,128)(2,1)S(1)} %slice.28.refs_1_.refs_0_), channel_id=1, source_target_pairs={{0,508},{4,0},{8,4},{12,8},{16,12},{20,16},{24,20},{28,24},{32,28}... | collective-permute-start | bytes 983048 | tf_op jit(solution)/shard_map/ppermute | solution.py:43
  20.0 0.0 copy-done.5
  20.0 0.6 reduce_sum.9
  20.6 0.7 divide_sqrt_fusion
  21.3 0.0 copy-done.6
  21.3 0.0 copy-done.4
  21.3 0.1 multiply_cosine_fusion.1
  21.4 0.3 fusion.1
  21.8 0.0 copy-done.2
  21.8 0.0 copy-done.1
  21.8 0.1 negate_convert_fusion
  21.9 0.1 broadcast_in_dim.8
  22.0 0.0 copy-start.3
  22.0 0.0 collective-permute-done.refs_2_.refs_1_
  22.0 6.0 %collective-permute-start.2 = (bf16[48,2048]{1,0:T(8,128)(2,1)S(1)}, bf16[48,2048]{1,0:T(8,128)(2,1)S(1)}, u32[]{:S(2)}, u32[]{:S(2)}) collective-permute-start(bf16[48,2048]{1,0:T(8,128)(2,1)S(1)} %collective-permute-done.refs_2_.refs_1_), channel_id=1, source_target_pairs={{0,508},{4,0},{8,4},{12,8},{16,12},{20,16},{24,20},{28,24},{32,28}... | collective-permute-start | bytes 589832 | tf_op jit(solution)/shard_map/ppermute | solution.py:43
  28.0 0.0 collective-permute-done.1.refs_3_.refs_2_
  28.0 7.0 %collective-permute-start.4 = (bf16[80,2048]{1,0:T(8,128)(2,1)S(1)}, bf16[80,2048]{1,0:T(8,128)(2,1)S(1)}, u32[]{:S(2)}, u32[]{:S(2)}) collective-permute-start(bf16[80,2048]{1,0:T(8,128)(2,1)S(1)} %collective-permute-done.1.refs_3_.refs_2_), channel_id=1, source_target_pairs={{0,508},{4,0},{8,4},{12,8},{16,12},{20,16},{24,20},{28,24},{32,28}... | collective-permute-start | bytes 983048 | tf_op jit(solution)/shard_map/ppermute | solution.py:43
  35.0 0.0 copy-done.3
  35.0 0.1 copy.12.offsets_ref
  35.1 0.0 collective-permute-done.2.refs_4_.refs_3_
  35.2 1.6 %terms.2 = (bf16[48,2048]{1,0:T(8,128)(2,1)S(1)}, bf16[48,2048]{1,0:T(8,128)(2,1)S(1)}, bf16[48,2048]{1,0:T(8,128)(2,1)S(1)}, bf16[48,2048]{1,0:T(8,128)(2,1)S(1)}) custom-call(s32[1]{0:T(128)} %bitcast.4.index_ref, s32[4,4,2]{2,1,0:T(4,128)S(1)} %copy.12.offsets_ref, bf16[48,2048]{1,0:T(8,128)(2,1)S(1)} %slice_bitcast_fusion.refs_0_, ...), custom_call_target="tpu_custom_call" | custom-call | flops 1024 | bytes 1024 | tf_op jit(solution)/shard_map/terms/pallas_call | solution.py:138
  36.8 3.7 %collective-permute-start.3 = (bf16[48,2048]{1,0:T(8,128)(2,1)S(1)}, bf16[48,2048]{1,0:T(8,128)(2,1)S(1)}, u32[]{:S(2)}, u32[]{:S(2)}) collective-permute-start(bf16[48,2048]{1,0:T(8,128)(2,1)S(1)} %get-tuple-element.23), channel_id=1, source_target_pairs={{0,1},{1,0},{2,3},{3,2},{4,5},{5,4},{6,7},{7,6},{8,9},{9,8},{10,11... | collective-permute-start | bytes 589832 | tf_op jit(solution)/shard_map/ppermute | solution.py:47
  40.5 1.0 %collective-permute-done.3 = bf16[48,2048]{1,0:T(8,128)(2,1)S(1)} collective-permute-done((bf16[48,2048]{1,0:T(8,128)(2,1)S(1)}, bf16[48,2048]{1,0:T(8,128)(2,1)S(1)}, u32[]{:S(2)}, u32[]{:S(2)}) %collective-permute-start.3) | collective-permute-done | bytes 196640 | tf_op jit(solution)/shard_map/ppermute | solution.py:47
  41.6 0.0 collective-permute-done.4.refs_4_
  41.6 2.2 %terms.3 = (bf16[80,2048]{1,0:T(8,128)(2,1)S(1)}, bf16[80,2048]{1,0:T(8,128)(2,1)S(1)}, bf16[208,2048]{1,0:T(8,128)(2,1)S(1)}) custom-call(s32[1]{0:T(128)} %bitcast.4.index_ref, s32[4,4,2]{2,1,0:T(4,128)S(1)} %copy.12.offsets_ref, bf16[80,2048]{1,0:T(8,128)(2,1)S(1)} %slice.28.refs_1_.refs_0_, bf16[48,2048]{1,0:T(8,128)(2,1)S(1)} %collective-permute-done.refs_2_.refs_1_, ...), custom_call_target="tpu_custom_call" | custom-call | flops 1024 | bytes 1024 | tf_op jit(solution)/shard_map/terms/pallas_call | solution.py:138
  43.8 3.3 %collective-permute-start.5 = (bf16[208,2048]{1,0:T(8,128)(2,1)S(1)}, bf16[208,2048]{1,0:T(8,128)(2,1)S(1)}, u32[]{:S(2)}, u32[]{:S(2)}) collective-permute-start(bf16[208,2048]{1,0:T(8,128)(2,1)S(1)} %get-tuple-element.27), channel_id=1, source_target_pairs={{0,1},{1,0},{2,3},{3,2},{4,5},{5,4},{6,7},{7,6},{8,9},{9,8},{10,11... | collective-permute-start | bytes 2555912 | tf_op jit(solution)/shard_map/ppermute | solution.py:47
  47.0 0.1 add_convert_fusion
  47.1 4.5 %collective-permute-start.6 = (bf16[48,2048]{1,0:T(8,128)(2,1)S(1)}, bf16[48,2048]{1,0:T(8,128)(2,1)S(1)}, u32[]{:S(2)}, u32[]{:S(2)}) collective-permute-start(bf16[48,2048]{1,0:T(8,128)(2,1)S(1)} %add_convert_fusion), channel_id=1, source_target_pairs={{0,2},{1,3},{2,0},{3,1},{4,6},{5,7},{6,4},{7,5},{8,10},{9,11},{10,... | collective-permute-start | bytes 589832 | tf_op jit(solution)/shard_map/ppermute | solution.py:51
  51.6 0.0 collective-permute-done.5.refs_2_
  51.6 0.0 copy-start
  51.6 0.1 add_convert_fusion.1
  51.8 2.3 %collective-permute-start.8 = (bf16[80,1024]{1,0:T(8,128)(2,1)S(1)}, bf16[80,1024]{1,0:T(8,128)(2,1)S(1)}, u32[]{:S(2)}, u32[]{:S(2)}) collective-permute-start(bf16[80,1024]{1,0:T(8,128)(2,1)S(1)} %get-tuple-element.31), channel_id=1, source_target_pairs={{0,2},{1,3},{2,0},{3,1},{4,6},{5,7},{6,4},{7,5},{8,10},{9,11},{10,... | collective-permute-start | bytes 491528 | tf_op jit(solution)/shard_map/ppermute | solution.py:51
  54.0 4.5 %collective-permute-start.7 = (bf16[80,1024]{1,0:T(8,128)(2,1)S(1)}, bf16[80,1024]{1,0:T(8,128)(2,1)S(1)}, u32[]{:S(2)}, u32[]{:S(2)}) collective-permute-start(bf16[80,1024]{1,0:T(8,128)(2,1)S(1)} %get-tuple-element.32), channel_id=1, source_target_pairs={{0,2},{1,3},{2,0},{3,1},{4,6},{5,7},{6,4},{7,5},{8,10},{9,11},{10,... | collective-permute-start | bytes 491528 | tf_op jit(solution)/shard_map/ppermute | solution.py:51
  58.6 0.0 collective-permute-done.6.refs_3_
  58.6 2.1 %collective-permute-done.8.refs_4_ = bf16[80,1024]{1,0:T(8,128)(2,1)S(1)} collective-permute-done((bf16[80,1024]{1,0:T(8,128)(2,1)S(1)}, bf16[80,1024]{1,0:T(8,128)(2,1)S(1)}, u32[]{:S(2)}, u32[]{:S(2)}) %collective-permute-start.8) | collective-permute-done | bytes 163872 | tf_op jit(solution)/shard_map/ppermute | solution.py:51
  60.7 0.0 copy-done
  60.7 2.3 %spots.2.refs_5_ = bf16[128,2048]{1,0:T(8,128)(2,1)} custom-call(bf16[768,256]{1,0:T(8,128)(2,1)S(1)} %bitcast.9, bf16[256,256]{1,0:T(8,128)(2,1)S(1)} %copy-done, f32[7,2048]{1,0:T(8,128)S(1)} %pad_maximum_fusion.column_ref, bf16[48,2048]{1,0:T(8,128)(2,1)S(1)} %get-tuple-element.22.refs_0_, bf16[80,2048]{1,0:T(8,128)(2,1)S(1)} %get-tuple-element.26.refs_1_, ...), custom_call_target="tpu_custom_call" | custom-call | flops 1024 | bytes 1024 | tf_op jit(solution)/shard_map/spots/pallas_call | solution.py:228
  62.9 1.2 %collective-permute-done.7.refs_4_ = bf16[80,1024]{1,0:T(8,128)(2,1)S(1)} collective-permute-done((bf16[80,1024]{1,0:T(8,128)(2,1)S(1)}, bf16[80,1024]{1,0:T(8,128)(2,1)S(1)}, u32[]{:S(2)}, u32[]{:S(2)}) %collective-permute-start.7) | collective-permute-done | bytes 163872 | tf_op jit(solution)/shard_map/ppermute | solution.py:51
  64.2 2.3 %spots.3 = bf16[128,2048]{1,0:T(8,128)(2,1)} custom-call(bf16[768,256]{1,0:T(8,128)(2,1)S(1)} %bitcast.10, bf16[256,256]{1,0:T(8,128)(2,1)S(1)} %copy-done, f32[7,2048]{1,0:T(8,128)S(1)} %pad_maximum_fusion.column_ref, bf16[48,2048]{1,0:T(8,128)(2,1)S(1)} %get-tuple-element.22.refs_0_, ...), custom_call_target="tpu_custom_call", output_to_operand_aliasing={{}: (8, {})} | custom-call | flops 1024 | bytes 1024 | tf_op jit(solution)/shard_map/spots/pallas_call | solution.py:228
  (5 shorter events, 0.1 us)
Async XLA Ops:
  0.9 21.1 %collective-permute-start = (bf16[48,2048]{1,0:T(8,128)(2,1)S(1)}, bf16[48,2048]{1,0:T(8,128)(2,1)S(1)}, u32[]{:S(2)}, u32[]{:S(2)}) collective-permute-start(bf16[48,2048]{1,0:T(8,128)(2,1)S(1)} %slice_bitcast_fusion.refs_0_), channel_id=1, source_target_pairs={{0,508},{4,0},{8,4},{12,8},{16,12},{20,16},{24,20},{28,24},{32,28}... | collective-permute-start | bytes 589832 | tf_op jit(solution)/shard_map/ppermute | solution.py:43
  16.1 3.9 %copy-start.5 = (f32[3]{0:T(128)S(1)}, f32[3]{0:T(128)}, u32[]{:S(2)}) copy-start(f32[3]{0:T(128)} %param.14) | copy-start | bytes 40
  16.1 5.2 %copy-start.6 = (s32[1,16]{1,0:T(1,128)S(1)}, s32[1,16]{1,0:T(1,128)}, u32[]{:S(2)}) copy-start(s32[1,16]{1,0:T(1,128)} %param.12) | copy-start | bytes 196
  16.1 5.2 %copy-start.4 = (f32[3]{0:T(128)S(1)}, f32[3]{0:T(128)}, u32[]{:S(2)}) copy-start(f32[3]{0:T(128)} %param.13) | copy-start | bytes 40
  16.1 5.6 %copy-start.2 = (f32[128,128]{1,0:T(8,128)S(1)}, f32[128,128]{1,0:T(8,128)}, u32[]{:S(2)}) copy-start(f32[128,128]{1,0:T(8,128)} %constant.35) | copy-start | bytes 196612
  17.2 4.6 %copy-start.1 = (f32[128,128]{1,0:T(8,128)S(1)}, f32[128,128]{1,0:T(8,128)}, u32[]{:S(2)}) copy-start(f32[128,128]{1,0:T(8,128)} %constant.36) | copy-start | bytes 196612
  17.2 10.8 %collective-permute-start.1 = (bf16[80,2048]{1,0:T(8,128)(2,1)S(1)}, bf16[80,2048]{1,0:T(8,128)(2,1)S(1)}, u32[]{:S(2)}, u32[]{:S(2)}) collective-permute-start(bf16[80,2048]{1,0:T(8,128)(2,1)S(1)} %slice.28.refs_1_.refs_0_), channel_id=1, source_target_pairs={{0,508},{4,0},{8,4},{12,8},{16,12},{20,16},{24,20},{28,24},{32,28}... | collective-permute-start | bytes 983048 | tf_op jit(solution)/shard_map/ppermute | solution.py:43
  22.0 13.0 %copy-start.3 = (s32[4,4,2]{1,2,0:T(2,128)S(1)}, s32[4,4,2]{1,2,0:T(2,128)}, u32[]{:S(2)}) copy-start(s32[4,4,2]{1,2,0:T(2,128)} %param.11) | copy-start | bytes 388
  22.0 13.1 %collective-permute-start.2 = (bf16[48,2048]{1,0:T(8,128)(2,1)S(1)}, bf16[48,2048]{1,0:T(8,128)(2,1)S(1)}, u32[]{:S(2)}, u32[]{:S(2)}) collective-permute-start(bf16[48,2048]{1,0:T(8,128)(2,1)S(1)} %collective-permute-done.refs_2_.refs_1_), channel_id=1, source_target_pairs={{0,508},{4,0},{8,4},{12,8},{16,12},{20,16},{24,20},{28,24},{32,28}... | collective-permute-start | bytes 589832 | tf_op jit(solution)/shard_map/ppermute | solution.py:43
  28.0 13.6 %collective-permute-start.4 = (bf16[80,2048]{1,0:T(8,128)(2,1)S(1)}, bf16[80,2048]{1,0:T(8,128)(2,1)S(1)}, u32[]{:S(2)}, u32[]{:S(2)}) collective-permute-start(bf16[80,2048]{1,0:T(8,128)(2,1)S(1)} %collective-permute-done.1.refs_3_.refs_2_), channel_id=1, source_target_pairs={{0,508},{4,0},{8,4},{12,8},{16,12},{20,16},{24,20},{28,24},{32,28}... | collective-permute-start | bytes 983048 | tf_op jit(solution)/shard_map/ppermute | solution.py:43
  36.8 4.8 %collective-permute-start.3 = (bf16[48,2048]{1,0:T(8,128)(2,1)S(1)}, bf16[48,2048]{1,0:T(8,128)(2,1)S(1)}, u32[]{:S(2)}, u32[]{:S(2)}) collective-permute-start(bf16[48,2048]{1,0:T(8,128)(2,1)S(1)} %get-tuple-element.23), channel_id=1, source_target_pairs={{0,1},{1,0},{2,3},{3,2},{4,5},{5,4},{6,7},{7,6},{8,9},{9,8},{10,11... | collective-permute-start | bytes 589832 | tf_op jit(solution)/shard_map/ppermute | solution.py:47
  43.8 7.9 %collective-permute-start.5 = (bf16[208,2048]{1,0:T(8,128)(2,1)S(1)}, bf16[208,2048]{1,0:T(8,128)(2,1)S(1)}, u32[]{:S(2)}, u32[]{:S(2)}) collective-permute-start(bf16[208,2048]{1,0:T(8,128)(2,1)S(1)} %get-tuple-element.27), channel_id=1, source_target_pairs={{0,1},{1,0},{2,3},{3,2},{4,5},{5,4},{6,7},{7,6},{8,9},{9,8},{10,11... | collective-permute-start | bytes 2555912 | tf_op jit(solution)/shard_map/ppermute | solution.py:47
  47.1 11.5 %collective-permute-start.6 = (bf16[48,2048]{1,0:T(8,128)(2,1)S(1)}, bf16[48,2048]{1,0:T(8,128)(2,1)S(1)}, u32[]{:S(2)}, u32[]{:S(2)}) collective-permute-start(bf16[48,2048]{1,0:T(8,128)(2,1)S(1)} %add_convert_fusion), channel_id=1, source_target_pairs={{0,2},{1,3},{2,0},{3,1},{4,6},{5,7},{6,4},{7,5},{8,10},{9,11},{10,... | collective-permute-start | bytes 589832 | tf_op jit(solution)/shard_map/ppermute | solution.py:51
  51.6 9.0 %copy-start = (bf16[256,256]{1,0:T(8,128)(2,1)S(1)}, bf16[256,256]{1,0:T(8,128)(2,1)}, u32[]{:S(2)}) copy-start(bf16[256,256]{1,0:T(8,128)(2,1)} %constant.32.clone.right_ref) | copy-start | bytes 393220
  51.8 8.9 %collective-permute-start.8 = (bf16[80,1024]{1,0:T(8,128)(2,1)S(1)}, bf16[80,1024]{1,0:T(8,128)(2,1)S(1)}, u32[]{:S(2)}, u32[]{:S(2)}) collective-permute-start(bf16[80,1024]{1,0:T(8,128)(2,1)S(1)} %get-tuple-element.31), channel_id=1, source_target_pairs={{0,2},{1,3},{2,0},{3,1},{4,6},{5,7},{6,4},{7,5},{8,10},{9,11},{10,... | collective-permute-start | bytes 491528 | tf_op jit(solution)/shard_map/ppermute | solution.py:51
  54.0 10.1 %collective-permute-start.7 = (bf16[80,1024]{1,0:T(8,128)(2,1)S(1)}, bf16[80,1024]{1,0:T(8,128)(2,1)S(1)}, u32[]{:S(2)}, u32[]{:S(2)}) collective-permute-start(bf16[80,1024]{1,0:T(8,128)(2,1)S(1)} %get-tuple-element.32), channel_id=1, source_target_pairs={{0,2},{1,3},{2,0},{3,1},{4,6},{5,7},{6,4},{7,5},{8,10},{9,11},{10,... | collective-permute-start | bytes 491528 | tf_op jit(solution)/shard_map/ppermute | solution.py:51
